TPU v7x, 256 devices: a whole 4x4x8 slice. The times are simulated.
256 devices in a mesh: section: 16 (over z, x_hi), blk: 16 (over x_lo, y, core).
Axes of the slice: x: 4 (x_hi: 2, x_lo: 2; x = x_hi * 2 + x_lo), y: 4, z: 8, core: 2. Of those that a mesh axis runs over, the one named last changes fastest.
Arguments:
- states: bfloat16 [16, 2048, 1216], P('section', 'blk'), may hold values from -6 to 6
- image_weight: bfloat16 [16, 1216, 3648], P('section'), may hold values from -0.15625 to 0.15625
- text_weight: bfloat16 [16, 1216, 2432], P('section', None, 'blk'), may hold values from -0.15625 to 0.15625
- text_states: bfloat16 [16, 256, 1216], P('section'), may hold values from -6 to 6
- stale_cache: bfloat16 [16, 2, 2048, 2432], P('section', None, 'blk'), may hold values from -3 to 3
- modulation: float32 [28, 16, 5, 1216], P(None, 'section'), may hold values from -4 to 4
- query_gain: float32 [16, 64], P('section'), may hold values from 0.5 to 3
- key_gain: float32 [16, 64], P('section'), may hold values from 0.5 to 3
- text_gain: float32 [16, 64], P('section'), may hold values from 0.5 to 3
- timestep: int32 [16], P('section'), may hold values from 0 to 27
- layer_patch_index: int32 [16], P('section'), may hold values from 0 to 1
Outputs:
- next_states: bfloat16 [16, 2048, 1216], P('section', 'blk')
- fresh_entries: bfloat16 [16, 2048, 2432], P('section', 'blk')
Inputs may be any that keep to these rules, and one draw needn't show every extreme that they name: `timestep`: index of a row of the modulation table. `layer_patch_index`: a patch number.
All inputs are finite; a program needn't handle non-finite values.
Results may differ from a plain program's by a relative error of at most 0.0055.
Values may be sent and summed in bfloat16 or wider, within the bound.
A program may use at most 192 MiB of HBM per device.

v0:
```python
import jax
import jax.numpy as jnp
from jax import lax
from jax.sharding import PartitionSpec as P


def passed_along(value, axis, steps):
    count = lax.axis_size(axis)
    pairs = [(source, (source + steps) % count) for source in range(count)]
    return lax.ppermute(value, axis, pairs)


def layer_norm(values):
    center = values - jnp.mean(values, axis=-1, keepdims=True)
    return center * lax.rsqrt(jnp.mean(center * center, axis=-1, keepdims=True) + 1e-06)


def head_norm(values, head_gain_table):
    rows_n = values.shape[0]
    size_head = head_gain_table.shape[0]
    per_head = values.reshape(rows_n, -1, size_head)
    scaled = (
        per_head
        * lax.rsqrt(jnp.mean(per_head * per_head, axis=-1, keepdims=True) + 1e-06)
        * head_gain_table
    )
    return scaled.reshape(rows_n, -1)


def partial_sums(queries, keys_block, size_head):
    attn_width = queries.shape[1]
    attention_channels = attn_width // size_head
    query_rows = queries.shape[0]
    key_rows = keys_block.shape[0]
    asking_channel_lines = queries.reshape(query_rows, attention_channels, size_head)
    lookup_channel_lines = keys_block[:, :attn_width].reshape(
        key_rows, attention_channels, size_head
    )
    value_head_rows = keys_block[:, attn_width:].reshape(key_rows, attention_channels, size_head)
    scores = (
        jnp.einsum(
            "apf,ipf->pai",
            asking_channel_lines,
            lookup_channel_lines,
            preferred_element_type=jnp.float32,
        )
        * 0.125
    )
    elementwise_powers = jnp.exp(scores)
    totals = jnp.sum(elementwise_powers, axis=2).T
    weighted = jnp.einsum(
        "ckq,qcw->kcw",
        elementwise_powers.astype(jnp.bfloat16),
        value_head_rows,
        preferred_element_type=jnp.float32,
    )
    return (weighted.reshape(query_rows, attn_width), totals)


def body(
    states,
    image_weight,
    text_weight,
    text_states,
    stale_cache,
    modulation,
    query_gain,
    key_gain,
    text_gain,
    timestep,
    layer_patch_index,
):
    current = states[0]
    size_head = query_gain.shape[1]
    attn_width = current.shape[1]
    rows_n = current.shape[0]
    patch_count = stale_cache.shape[1]
    chosen = jnp.arange(modulation.shape[0], dtype=jnp.int32) == timestep[0]
    modulate = jnp.sum(jnp.where(chosen[:, None, None], modulation[:, 0], 0.0), axis=0)
    normed = (layer_norm(current.astype(jnp.float32)) * (1.0 + modulate[1]) + modulate[0]).astype(
        jnp.bfloat16
    )
    project = jnp.dot(normed, image_weight[0], preferred_element_type=jnp.float32)
    queries = head_norm(project[:, :attn_width], query_gain[0]).astype(jnp.bfloat16)
    keys_now = head_norm(project[:, attn_width : 2 * attn_width], key_gain[0]).astype(jnp.bfloat16)
    values_now = project[:, 2 * attn_width :].astype(jnp.bfloat16)
    fresh = jnp.concatenate([keys_now, values_now], axis=1)
    text_normed = (
        layer_norm(text_states[0].astype(jnp.float32)) * (1.0 + modulate[4]) + modulate[3]
    ).astype(jnp.bfloat16)
    text_part = jnp.dot(text_normed, text_weight[0], preferred_element_type=jnp.float32).astype(
        jnp.bfloat16
    )
    text_raw = lax.all_gather(text_part, "blk", axis=1, tiled=True)
    text_key = head_norm(text_raw[:, :attn_width].astype(jnp.float32), text_gain[0]).astype(
        jnp.bfloat16
    )
    text_entries = jnp.concatenate([text_key, text_raw[:, attn_width:]], axis=1)
    text_weighted, text_score_sums = partial_sums(queries, text_entries, size_head)
    slot_mask = jnp.arange(patch_count, dtype=jnp.int32) == layer_patch_index[0]
    merged = jnp.where(slot_mask[:, None, None], fresh[None], stale_cache[0]).reshape(
        -1, 2 * attn_width
    )
    extra_sum, extra_total = partial_sums(
        queries, lax.all_gather(merged, "blk", axis=0, tiled=True), size_head
    )
    weighted = text_weighted + extra_sum
    totals = text_score_sums + extra_total
    attended = (weighted.reshape(rows_n, -1, size_head) / totals[:, :, None]).reshape(
        rows_n, attn_width
    )
    updated = (current.astype(jnp.float32) + modulate[2] * attended).astype(jnp.bfloat16)
    next_states = passed_along(updated[None], "section", 1)
    return (next_states, fresh[None])


def solution(mesh):
    in_specs = (
        P("section", "blk", None),
        P("section", None, None),
        P("section", None, "blk"),
        P("section", None, None),
        P("section", None, "blk", None),
        P(None, "section", None, None),
        P("section", None),
        P("section", None),
        P("section", None),
        P("section"),
        P("section"),
    )
    out_specs = (P("section", "blk", None), P("section", "blk", None))
    return jax.shard_map(body, mesh=mesh, in_specs=in_specs, out_specs=out_specs, check_vma=False)
```

profile of v0, /device:TPU:1, one launch (start us, length us, event | category | flops | bytes accessed | tf_op | source)
XLA Modules:
  0.0 243.7 jit_solution(12906532583522560896)
XLA Ops:
  7.2 0.0 copy-start
  7.2 0.0 copy-start.5
  7.2 0.0 all-gather.3.cloned.1.call-start
  8.0 1.3 fusion.22
  9.3 0.0 copy-start.2
  9.3 0.1 slice_reduce_fusion.2
  9.4 1.3 convert_reduce_fusion
  10.6 0.0 copy-done.5
  10.6 0.2 fusion.19
  10.9 0.0 copy-done
  10.9 1.2 convolution_convert_fusion
  12.1 0.0 all-gather.3.cloned.1.call-update
  12.1 0.0 all-gather.5.cloned.1.call-start
  12.2 0.2 convert_reduce_fusion.1
  12.4 0.2 fusion.29
  12.5 7.8 %fusion.5 = f32[128,3648]{0,1:T(8,128)S(1)} fusion(bf16[1,1216,3648]{2,1,0:T(8,128)(2,1)} %param.12, bf16[1,128,1216]{1,2,0:T(8,128)(2,1)S(1)} %copy-done.2, f32[1216]{0:T(1024)S(1)} %get-tuple-element.7, f32[1216]{0:T(1024)S(1)} %get-tuple-element.8, f32[128]{0:T(128)S(1)} %add_rsqrt_fusion.4, f32[128]{0:T(128)S(1)} %broadcast_multiply_fusion.1), kind=kOutput, calls=%fused_computation.5 | convolution fusion | flops 1136541696 | bytes 11061760 | tf_op jit(solution)/shard_map/dot_general | solution.py:83
  20.3 0.0 copy-start.6
  20.3 2.6 %copy.16 = bf16[256,2432]{0,1:T(8,128)(2,1)} copy(bf16[256,2432]{1,0:T(8,128)(2,1)} %bitcast.97) | data formatting | bytes 2490368 | tf_op jit(solution)/shard_map/squeeze | solution.py:101
  23.0 0.1 mul.192
  23.1 0.9 slice_multiply_fusion.1
  24.0 1.1 reduce_sum.97
  25.1 0.1 reduce_sum.95
  25.2 0.1 mul.214
  26.0 0.4 fusion.36
  26.4 0.1 broadcast_bitcast_fusion
  26.5 0.9 fusion.52
  27.4 6.4 %broadcast_in_dim.56 = bf16[2,128,2432]{1,0,2:T(2,128)(2,1)S(1)} broadcast(bf16[128,2432]{0,1:T(8,128)(2,1)S(1)} %get-tuple-element.18), dimensions={1,2} | broadcast | bytes 1867776 | tf_op jit(solution)/shard_map/jit(_where)/broadcast_in_dim | solution.py:101
  33.8 0.0 copy-start.8
  33.8 1.2 bitcast_select_fusion
  35.1 0.0 all-gather.5.cloned.1.call-update
  35.1 0.1 mul.202
  35.2 16.6 %all-gather.3.cloned.1.call-done = bf16[256,2432]{0,1:T(8,128)(2,1)} async-done(((bf16[256,152]{0,1:T(8,128)(2,1)}), bf16[256,2432]{0,1:T(8,128)(2,1)}) %all-gather.3.cloned.1.call-update) | async-done | bytes 1245200 | tf_op jit(solution)/shard_map/all_gather | solution.py:94
  51.8 1.3 convert_multiply_fusion.1
  53.1 0.1 reduce_sum.96
  53.2 0.1 copy-done.4
  53.3 0.3 fusion.12
  53.6 0.7 fusion.7
  54.3 116.4 %all-gather.5.cloned.1.call-done = bf16[4096,2432]{0,1:T(8,128)(2,1)} async-done(((bf16[256,2432]{0,1:T(8,128)(2,1)}), bf16[4096,2432]{0,1:T(8,128)(2,1)}) %all-gather.5.cloned.1.call-update) | async-done | bytes 19922960 | tf_op jit(solution)/shard_map/all_gather | solution.py:105
  170.7 15.6 %fusion.53 = (bf16[4096,1216]{0,1:T(8,128)(2,1)}, bf16[4096,1216]{0,1:T(8,128)(2,1)}) fusion(bf16[4096,2432]{0,1:T(8,128)(2,1)} %all-gather.5.cloned.1.call-done), kind=kLoop, calls=%fused_computation.87 | loop fusion | bytes 39845888 | tf_op jit(solution)/shard_map/slice | solution.py:36
  186.2 18.2 %fusion = (f32[19,128]{1,0:T(8,128)S(1)}, f32[19,128,4096]{2,1,0:T(8,128)}) fusion(bf16[128,19,64]{0,2,1:T(8,128)(2,1)S(1)} %bitcast.92, bf16[4096,19,64]{0,2,1:T(8,128)(2,1)} %bitcast.88), kind=kOutput, calls=%fused_computation.1 | convolution fusion | flops 1294988928 | bytes 50128384 | tf_op jit(solution)/shard_map/apf,ipf->pai/dot_general | solution.py:41
  204.4 18.3 %fusion.2 = f32[19,64,128]{2,1,0:T(8,128)S(1)} fusion(bf16[4096,19,64]{0,2,1:T(8,128)(2,1)} %bitcast.87, f32[19,128,4096]{2,1,0:T(8,128)} %get-tuple-element.22), kind=kOutput, calls=%fused_computation.3 | convolution fusion | flops 1294991360 | bytes 50429952 | tf_op jit(solution)/shard_map/ckq,qcw->kcw/dot_general | solution.py:51
  222.7 0.0 copy-start.1
  222.7 0.6 fusion.10
  223.3 0.3 fusion.30
  223.6 2.5 %collective-permute-start = (bf16[1,128,1216]{1,2,0:T(8,128)(2,1)S(1)}, bf16[1,128,1216]{1,2,0:T(8,128)(2,1)S(1)}, u32[]{:S(2)}, u32[]{:S(2)}) collective-permute-start(bf16[1,128,1216]{1,2,0:T(8,128)(2,1)S(1)} %fusion.30), channel_id=1, source_target_pairs={{0,16},{16,32},{32,48},{48,64},{64,80},{80,96},{96,112},{112,128},... | collective-permute-start | bytes 933896 | tf_op jit(solution)/shard_map/ppermute | solution.py:10
  226.1 2.1 copy.17
  228.2 8.0 %collective-permute-done = bf16[1,128,1216]{1,2,0:T(8,128)(2,1)S(1)} collective-permute-done((bf16[1,128,1216]{1,2,0:T(8,128)(2,1)S(1)}, bf16[1,128,1216]{1,2,0:T(8,128)(2,1)S(1)}, u32[]{:S(2)}, u32[]{:S(2)}) %collective-permute-start) | collective-permute-done | bytes 311328 | tf_op jit(solution)/shard_map/ppermute | solution.py:10
  236.2 0.7 copy.24
  (24 shorter events, 0.1 us)
Async XLA Ops:
  7.2 3.7 %copy-start = (bf16[1,1216,152]{1,2,0:T(8,128)(2,1)S(1)}, bf16[1,1216,152]{1,2,0:T(8,128)(2,1)}, u32[]{:S(2)}) copy-start(bf16[1,1216,152]{1,2,0:T(8,128)(2,1)} %param.13) | copy-start | bytes 1108996
  7.2 3.5 %copy-start.5 = (bf16[1,256,1216]{1,2,0:T(8,128)(2,1)S(1)}, bf16[1,256,1216]{1,2,0:T(8,128)(2,1)}, u32[]{:S(2)}) copy-start(bf16[1,256,1216]{1,2,0:T(8,128)(2,1)} %param.14) | copy-start | bytes 1867780
  7.2 44.6 %all-gather.3.cloned.1.call-start = ((), (), s32[]{:S(2)}) async-start(), calls=%async_computation | async-start | bytes 1323008 | tf_op jit(solution)/shard_map/all_gather | solution.py:94
  9.3 2.9 %copy-start.2 = (bf16[1,128,1216]{1,2,0:T(8,128)(2,1)S(1)}, bf16[1,128,1216]{1,2,0:T(8,128)(2,1)}, u32[]{:S(2)}) copy-start(bf16[1,128,1216]{1,2,0:T(8,128)(2,1)} %param.11) | copy-start | bytes 933892
  12.1 158.6 %all-gather.5.cloned.1.call-start = ((), (), s32[]{:S(2)}) async-start(), calls=%async_computation.1 | async-start | bytes 21168128 | tf_op jit(solution)/shard_map/all_gather | solution.py:105
  20.3 2.7 %copy-start.6 = (f32[1,64]{1,0:T(1,128)S(1)}, f32[1,64]{1,0:T(1,128)}, u32[]{:S(2)}) copy-start(f32[1,64]{1,0:T(1,128)} %param.17) | copy-start | bytes 772
  23.1 2.1 copy-start.7
  26.5 7.4 %copy-start.3 = (bf16[256,2432]{0,1:T(8,128)(2,1)S(1)}, bf16[256,2432]{0,1:T(8,128)(2,1)}, u32[]{:S(2)}) copy-start(bf16[256,2432]{0,1:T(8,128)(2,1)} %copy.16) | copy-start | bytes 3735556
  33.8 1.3 copy-start.8
  51.8 1.5 copy-start.4
  204.4 18.3 %slice-start = ((bf16[256,2432]{0,1:T(8,128)(2,1)}), bf16[256,1216]{0,1:T(8,128)(2,1)S(1)}, s32[]{:S(2)}) async-start(bf16[256,2432]{0,1:T(8,128)(2,1)} %all-gather.3.cloned.1.call-done), calls=%async_computation.2 | async-start | bytes 1245184 | tf_op jit(solution)/shard_map/slice | solution.py:98
  222.7 14.2 %copy-start.1 = (bf16[1,1216,152]{1,2,0:T(8,128)(2,1)S(1)}, bf16[1,1216,152]{1,2,0:T(8,128)(2,1)}, u32[]{:S(2)}) copy-start(bf16[1,1216,152]{1,2,0:T(8,128)(2,1)} %param.13) | copy-start | bytes 1108996
  223.6 12.6 %collective-permute-start = (bf16[1,128,1216]{1,2,0:T(8,128)(2,1)S(1)}, bf16[1,128,1216]{1,2,0:T(8,128)(2,1)S(1)}, u32[]{:S(2)}, u32[]{:S(2)}) collective-permute-start(bf16[1,128,1216]{1,2,0:T(8,128)(2,1)S(1)} %fusion.30), channel_id=1, source_target_pairs={{0,16},{16,32},{32,48},{48,64},{64,80},{80,96},{96,112},{112,128},... | collective-permute-start | bytes 933896 | tf_op jit(solution)/shard_map/ppermute | solution.py:10
Sparse Core Ops, SparseCore 0:
  12.2 39.5 all-gather.2
  53.6 117.0 all-gather.4
where the time goes:
time: 244 us
  waiting for transfers between devices  141 us (58%)
  matrix products  46.7 us (19%)
  local copies, waits for them, and re-layouts  28 us (11%)
  between operations  15.7 us (6%)
  other arithmetic  9.81 us (4%)
  starting transfers between devices  2.56 us (1%)
    all_gather x1, waiting for transfers between devices, body(): lax.all_gather(merged, 'blk', axis=0, tiled=True)  116 us
    dot_general x2, matrix products, partial_sums(): jnp.einsum('ckq,qcw->kcw', elementwise_powers.astype(jnp.bfloat16), value...  18.9 us
    dot_general x2, matrix products, partial_sums(): jnp.einsum('apf,ipf->pai', asking_channel_lines, lookup_channel_lines, pr...  18.9 us
    all_gather x1, waiting for transfers between devices, body(): text_raw = lax.all_gather(text_part, 'blk', axis=1, tiled=True)  16.6 us
    slice x1, local copies, waits for them, and re-layouts, partial_sums(): keys_block[:, :attn_width].reshape(key_rows, attention_channels, size_head)  15.6 us
    ppermute x1, waiting for transfers between devices, passed_along(): return lax.ppermute(value, axis, pairs)  7.96 us
    dot_general x1, matrix products, body(): jnp.dot(normed, image_weight[0], preferred_element_type=jnp.float32)  7.77 us
    broadcast_in_dim x2, local copies, waits for them, and re-layouts, body(): jnp.where(slot_mask[:, None, None], fresh[None], stale_cache[0])  6.51 us
  transfers between devices with their start and end apart: 3, of which 3 were waited for; matrix products, arithmetic and copies ran while one was open for 11% of the time, Pallas kernels for 0%

commit v1 on v0

v1 whole, which is shorter than its diff:
```python
import functools

import jax
import jax.numpy as jnp
from jax import lax
from jax.experimental import pallas as pl
from jax.experimental.pallas import tpu as pltpu
from jax.sharding import PartitionSpec as P

MESH = pl.DeviceIdType.MESH
BF = jnp.bfloat16
F32 = jnp.float32

D = 1216
HEADS = 19
HD = 64
TOK = 128
TEXT = 256
BLK = 16
TEXT_COLS = 152
SPARE = 4
ROWS = BLK * TOK
SPARE_ROWS = SPARE * TOK
W_ROWS = 304
SPARE_GROUPS = ((0, 6, 3), (6, 6, 3), (12, 4, 4))
QT = 256


def low_half(rows):
    return lax.broadcasted_iota(jnp.int32, (rows, 128), 1) < HD


def swap_halves(value):
    return pltpu.roll(value, HD, axis=1)


def layer_norm(values):
    center = values - jnp.mean(values, axis=-1, keepdims=True)
    return center * lax.rsqrt(jnp.mean(center * center, axis=-1, keepdims=True) + 1e-06)


def pack_heads(source, sends):
    low = low_half(TOK)

    def tile(index):
        return source[:, 128 * index : 128 * index + 128].astype(F32)

    for head in range(HEADS):
        half = head // 2
        if head % 2 == 0:
            packed = jnp.where(low, tile(half), tile(9 + half))
        else:
            packed = swap_halves(jnp.where(low, tile(10 + half), tile(half)))
        packed = packed.astype(BF)
        if head < BLK:
            sends[head, 0] = packed
        else:
            first, count, _ = SPARE_GROUPS[head - BLK]
            for device in range(first, first + count):
                sends[device, 1] = packed


def kernel(
    sections,
    patch_ref,
    states_hbm,
    weight_hbm,
    text_weight_ref,
    text_hbm,
    stale_hbm,
    mod_ref,
    query_gain_ref,
    key_gain_ref,
    text_gain_ref,
    out_ref,
    fresh_hbm,
    states_v,
    weight_v,
    text_v,
    stale_v,
    entries_v,
    proj_v,
    fresh_v,
    kv_send,
    kv_recv,
    q_send,
    q_recv,
    q_spare,
    q_all,
    acc,
    text_send,
    text_recv,
    text_kv,
    gate_v,
    out_send,
    out_recv,
    prev_v,
    load_sem,
    weight_sem,
    kv_ssem,
    kv_rsem,
    q_ssem,
    q_rsem,
    spare_ssem,
    spare_rsem,
    text_ssem,
    text_ssem2,
    text_rsem,
    out_ssem,
    out_ssem2,
    out_rsem,
    prev_ssem,
    prev_rsem,
    fresh_sem,
):
    sec = lax.axis_index("section")
    me = lax.axis_index("blk")
    after = lax.rem(sec + 1, sections)
    before = lax.rem(sec + sections - 1, sections)

    load_stale = pltpu.make_async_copy(stale_hbm, stale_v, load_sem.at[0])
    load_states = pltpu.make_async_copy(states_hbm, states_v, load_sem.at[1])
    load_text = pltpu.make_async_copy(text_hbm, text_v, load_sem.at[2])
    load_stale.start()
    load_states.start()
    loads = []
    for part in range(D // W_ROWS):
        rows = pl.ds(part * W_ROWS, W_ROWS)
        loads.append(
            pltpu.make_async_copy(weight_hbm.at[rows], weight_v.at[rows], weight_sem.at[part])
        )
        loads[-1].start()
    load_text.start()

    barrier = pltpu.get_barrier_semaphore()

    @pl.loop(1, BLK)
    def _(step):
        pl.semaphore_signal(
            barrier, inc=1, device_id=(sec, lax.rem(me + step, BLK)), device_id_type=MESH
        )

    @pl.loop(0, BLK)
    def _(step):
        pl.semaphore_signal(
            barrier, inc=1, device_id=(before, lax.rem(me + step, BLK)), device_id_type=MESH
        )

    group = jnp.where(me < 6, 0, jnp.where(me < 12, 1, 2))
    per_device = jnp.where(me < 12, 3, 4)
    first_block = (me - 6 * group) * per_device
    spare_head = BLK + group

    def send_entries(kind):
        @pl.loop(1, BLK)
        def _(step):
            to = lax.rem(me + step, BLK)
            pltpu.make_async_remote_copy(
                src_ref=kv_send.at[kind, to],
                dst_ref=kv_recv.at[kind, me],
                send_sem=kv_ssem.at[kind],
                recv_sem=kv_rsem.at[kind, me],
                device_id=(sec, to),
                device_id_type=MESH,
            ).start()

        pltpu.make_async_copy(
            kv_send.at[kind, me], kv_recv.at[kind, me], kv_rsem.at[kind, me]
        ).start()

    load_stale.wait()
    first_worked = patch_ref[0] == 0
    for index in range(HEADS):
        cols = slice(128 * index, 128 * index + 128)
        entries_v[:, cols] = jnp.where(first_worked, stale_v[1, :, cols], stale_v[0, :, cols])
    pack_heads(entries_v, kv_send.at[0])
    pl.semaphore_wait(barrier, 2 * BLK - 1)
    send_entries(0)

    load_states.wait()
    prev_copy = pltpu.make_async_remote_copy(
        src_ref=states_v,
        dst_ref=prev_v,
        send_sem=prev_ssem,
        recv_sem=prev_rsem,
        device_id=(after, me),
        device_id_type=MESH,
    )
    prev_copy.start()

    normed = (
        layer_norm(states_v[...].astype(F32).T) * (1.0 + mod_ref[1:2, :]) + mod_ref[0:1, :]
    ).astype(BF)
    for load in loads:
        load.wait()

    block_ones = (
        (lax.broadcasted_iota(jnp.int32, (128, 128), 0) < HD)
        == (lax.broadcasted_iota(jnp.int32, (128, 128), 1) < HD)
    ).astype(BF)
    query_gain = query_gain_ref[...]
    key_gain = key_gain_ref[...]

    def project(first, last):
        proj_v[:, first:last] = jnp.dot(
            normed, weight_v[:, first:last], preferred_element_type=F32
        )

    def normed_tile(index):
        value = proj_v[:, 128 * index : 128 * index + 128]
        square = value * value
        high = square.astype(BF)
        low = (square - high.astype(F32)).astype(BF)
        mean = (
            jnp.dot(high, block_ones, preferred_element_type=F32)
            + jnp.dot(low, block_ones, preferred_element_type=F32)
        ) * (1.0 / HD)
        gain = jnp.concatenate(
            [
                query_gain if index < 10 else key_gain,
                query_gain if index < 9 else key_gain,
            ],
            axis=1,
        )
        return value * lax.rsqrt(mean + 1e-06) * gain

    low64 = low_half(HD)
    project(0, 1280)
    for index in range(10):
        value = normed_tile(index)
        if index == 9:
            proj_v[:, 128 * index : 128 * index + 128] = value
        top, bottom = value[:HD], value[HD:]
        even = jnp.where(low64, top, swap_halves(bottom))
        q_send[2 * index] = (even.astype(BF).astype(F32) * 0.125).astype(BF)
        if index < 9:
            odd = jnp.where(low64, swap_halves(top), bottom)
            q_send[2 * index + 1] = (odd.astype(BF).astype(F32) * 0.125).astype(BF)

    @pl.loop(1, BLK)
    def _(step):
        to = lax.rem(me + step, BLK)
        pltpu.make_async_remote_copy(
            src_ref=q_send.at[to],
            dst_ref=q_recv.at[me],
            send_sem=q_ssem,
            recv_sem=q_rsem,
            device_id=(sec, to),
            device_id_type=MESH,
        ).start()

    pltpu.make_async_copy(q_send.at[me], q_recv.at[me], q_rsem).start()

    def spare_query(index):
        first, _, size = SPARE_GROUPS[index]
        to = first + me // size
        slot = lax.rem(me, size)
        return to, pltpu.make_async_remote_copy(
            src_ref=q_send.at[BLK + index],
            dst_ref=q_spare.at[slot],
            send_sem=spare_ssem.at[index],
            recv_sem=spare_rsem.at[slot],
            device_id=(sec, to),
            device_id_type=MESH,
        ), pltpu.make_async_copy(
            q_send.at[BLK + index], q_spare.at[slot], spare_rsem.at[slot]
        )

    for index in range(3):
        to, remote, local = spare_query(index)
        pl.when(to != me)(remote.start)
        pl.when(to == me)(local.start)

    project(1280, 2432)
    project(2432, 3648)
    low = low_half(TOK)

    def swapped_tile(index):
        if index == 9 or index >= 19:
            return swap_halves(proj_v[:, 128 * index : 128 * index + 128])
        return swap_halves(normed_tile(index))

    left = swapped_tile(9)
    for index in range(HEADS):
        right = swapped_tile(10 + index)
        fresh_v[:, 128 * index : 128 * index + 128] = jnp.where(low, left, right).astype(BF)
        left = right
    fresh_copy = pltpu.make_async_copy(fresh_v, fresh_hbm, fresh_sem)
    fresh_copy.start()
    pack_heads(fresh_v, kv_send.at[1])
    send_entries(1)

    load_text.wait()
    text_normed = (
        layer_norm(text_v[...].astype(F32).T) * (1.0 + mod_ref[4:5, :]) + mod_ref[3:4, :]
    ).astype(BF)
    text_send[...] = (
        lax.dot_general(
            text_weight_ref[...],
            text_normed,
            (((1,), (1,)), ((), ())),
            preferred_element_type=F32,
        )
        .astype(BF)
        .astype(F32)
    )

    def text_main(step):
        unit = TEXT_COLS // 8 * me + step
        second = unit // TEXT_COLS
        head = (unit - TEXT_COLS * second) // 8
        to_row = pl.multiple_of(HD * second + 8 * lax.rem(unit, 8), 8)
        source = text_send.at[pl.ds(pl.multiple_of(8 * step, 8), 8)]
        target = text_recv.at[0, pl.ds(to_row, 8)]
        return (
            head,
            lambda: pltpu.make_async_remote_copy(
                src_ref=source,
                dst_ref=target,
                send_sem=text_ssem.at[step],
                recv_sem=text_rsem.at[0],
                device_id=(sec, head),
                device_id_type=MESH,
            ),
            lambda: pltpu.make_async_copy(source, target, text_rsem.at[0]),
        )

    @pl.loop(0, TEXT_COLS // 8)
    def _(step):
        head, remote, local = text_main(step)

        @pl.when(jnp.logical_and(head < BLK, head != me))
        def _():
            remote().start()

        @pl.when(head == me)
        def _():
            local().start()

    pieces = ((6, 112, 40, 0, 0), (7, 0, 24, 0, 40), (7, 24, 64, 1, 0), (7, 88, 64, 2, 0))
    second_half = me // 8

    def text_spare(number, step):
        _, row, rows, index, to_row = pieces[number]
        to = SPARE_GROUPS[index][0] + step
        source = text_send.at[pl.ds(row, rows)]
        target = text_recv.at[1, pl.ds(pl.multiple_of(HD * second_half + to_row, 8), rows)]
        return (
            to,
            lambda: pltpu.make_async_remote_copy(
                src_ref=source,
                dst_ref=target,
                send_sem=text_ssem2.at[number, step],
                recv_sem=text_rsem.at[1],
                device_id=(sec, to),
                device_id_type=MESH,
            ),
            lambda: pltpu.make_async_copy(source, target, text_rsem.at[1]),
        )

    for number in range(4):

        @pl.when(lax.rem(me, 8) == pieces[number][0])
        def _():
            @pl.loop(0, SPARE_GROUPS[pieces[number][3]][1])
            def _(step):
                to, remote, local = text_spare(number, step)

                @pl.when(to != me)
                def _():
                    remote().start()

                @pl.when(to == me)
                def _():
                    local().start()

    one = jnp.ones((1, 128), F32)
    low1 = low_half(1)
    gate_pad = jnp.concatenate([mod_ref[2:3, :], jnp.zeros((1, 64), F32)], axis=1)
    for head in range(HEADS):
        gate = gate_pad[:, 128 * (head // 2) : 128 * (head // 2) + 128]
        if head % 2 == 0:
            gate = swap_halves(jnp.broadcast_to(gate, (8, 128)))[0:1]
        gate_v[head : head + 1, :] = jnp.where(low1, one, gate)

    pltpu.make_async_copy(q_recv, q_recv, q_rsem).wait()

    def spread_queries(packed, row):
        value = packed.astype(F32)
        zero = jnp.zeros_like(value)
        q_all[pl.ds(row, HD)] = jnp.where(low64, value, zero).astype(BF)
        q_all[pl.ds(row + HD, HD)] = jnp.where(low64, swap_halves(value), zero).astype(BF)

    @pl.loop(0, BLK)
    def _(step):
        spread_queries(q_recv[step], pl.multiple_of(step * TOK, TOK))

    q_all[pl.ds(ROWS, SPARE_ROWS)] = jnp.zeros((SPARE_ROWS, 128), BF)
    for slot in range(SPARE):

        @pl.when(jnp.logical_and(slot < per_device, first_block + slot < BLK))
        def _():
            pltpu.make_async_copy(q_spare.at[slot], q_spare.at[slot], spare_rsem.at[slot]).wait()
            spread_queries(q_spare[slot], ROWS + slot * TOK)

    low256 = low_half(256)

    def attend(entries, first, rows):
        values = jnp.where(low256, jnp.ones((256, 128), F32), entries.astype(F32)).astype(BF)

        @pl.loop(0, rows // QT)
        def _(step):
            at = pl.ds(pl.multiple_of(first + step * QT, QT), QT)
            scores = lax.dot_general(
                q_all[at], entries, (((1,), (1,)), ((), ())), preferred_element_type=F32
            )
            powers = jnp.exp(scores).astype(BF)
            acc[at] += jnp.dot(powers, values, preferred_element_type=F32)

    acc[...] = jnp.zeros_like(acc)

    def attend_patch(kind):
        @pl.loop(0, BLK // 2)
        def _(step):
            pair = lax.rem(me // 2 + BLK // 2 - step, BLK // 2)
            for core in range(2):
                one_source = kv_recv.at[kind, 2 * pair + core]
                pltpu.make_async_copy(
                    one_source, one_source, kv_rsem.at[kind, 2 * pair + core]
                ).wait()
            for which, first, rows in ((0, 0, ROWS), (1, ROWS, SPARE_ROWS)):
                entries = kv_recv[kind, pl.ds(2 * pair, 2), which].reshape(256, 128)
                attend(entries, first, rows)

    attend_patch(0)

    text_gain = jnp.concatenate([text_gain_ref[...], jnp.ones((1, HD), F32)], axis=1)
    for which, first, rows in ((0, 0, ROWS), (1, ROWS, SPARE_ROWS)):
        pltpu.make_async_copy(
            text_recv.at[which], text_recv.at[which], text_rsem.at[which]
        ).wait()
        value = text_recv[which].T
        square = jnp.where(low256, value * value, 0.0)
        mean = jnp.sum(square, axis=1, keepdims=True) * (1.0 / HD)
        scaled = value * lax.rsqrt(mean + 1e-06) * text_gain
        text_kv[which] = jnp.where(low256, scaled, value).astype(BF)
        attend(text_kv[which], first, rows)

    attend_patch(1)

    def result_of(row, head):
        value = acc[pl.ds(row, TOK)] * gate_v[pl.ds(head, 1), :]
        turned = value.T
        return (turned[HD:] / turned[:HD]).astype(BF)

    def result_copy(slot, head, block, sem):
        return pltpu.make_async_remote_copy(
            src_ref=out_send.at[slot],
            dst_ref=out_recv.at[head],
            send_sem=sem,
            recv_sem=out_rsem,
            device_id=(after, block),
            device_id_type=MESH,
        )

    @pl.loop(0, BLK)
    def _(step):
        block = lax.rem(me + step, BLK)
        out_send[block] = result_of(pl.multiple_of(block * TOK, TOK), me)
        result_copy(block, me, block, out_ssem).start()

    for slot in range(SPARE):

        @pl.when(jnp.logical_and(slot < per_device, first_block + slot < BLK))
        def _():
            out_send[BLK + slot] = result_of(ROWS + slot * TOK, spare_head)
            result_copy(BLK + slot, spare_head, first_block + slot, out_ssem2.at[slot]).start()

    prev_copy.wait_recv()
    pltpu.make_async_copy(out_recv, out_recv, out_rsem).wait()
    for head in range(HEADS):
        rows = slice(HD * head, HD * head + HD)
        out_ref[rows, :] = (prev_v[rows, :].astype(F32) + out_recv[head].astype(F32)).astype(BF)

    fresh_copy.wait()
    prev_copy.wait_send()
    for kind in range(2):
        sent = kv_send.at[kind, pl.ds(0, BLK - 1)]
        pltpu.make_async_copy(sent, sent, kv_ssem.at[kind]).wait()
    sent = q_send.at[pl.ds(0, BLK - 1)]
    pltpu.make_async_copy(sent, sent, q_ssem).wait()
    for index in range(3):
        to, remote, _ = spare_query(index)
        pl.when(to != me)(remote.wait_send)

    @pl.loop(0, TEXT_COLS // 8)
    def _(step):
        head, remote, _ = text_main(step)

        @pl.when(jnp.logical_and(head < BLK, head != me))
        def _():
            remote().wait_send()

    for number in range(4):

        @pl.when(lax.rem(me, 8) == pieces[number][0])
        def _():
            @pl.loop(0, SPARE_GROUPS[pieces[number][3]][1])
            def _(step):
                to, remote, _ = text_spare(number, step)

                @pl.when(to != me)
                def _():
                    remote().wait_send()

    sent = out_send.at[pl.ds(0, BLK)]
    pltpu.make_async_copy(sent, sent, out_ssem).wait()
    for slot in range(SPARE):

        @pl.when(jnp.logical_and(slot < per_device, first_block + slot < BLK))
        def _():
            result_copy(BLK + slot, spare_head, first_block + slot, out_ssem2.at[slot]).wait_send()


def body(
    sections,
    states,
    image_weight,
    text_weight,
    text_states,
    stale_cache,
    modulation,
    query_gain,
    key_gain,
    text_gain,
    timestep,
    layer_patch_index,
):
    modulate = lax.dynamic_index_in_dim(modulation[:, 0], timestep[0], 0, keepdims=False)
    vmem = pl.BlockSpec(memory_space=pltpu.VMEM)
    anywhere = pl.BlockSpec(memory_space=pl.ANY)
    dma = pltpu.SemaphoreType.DMA
    next_states, fresh = pl.pallas_call(
        functools.partial(kernel, sections),
        out_shape=(
            jax.ShapeDtypeStruct((D, TOK), BF),
            jax.ShapeDtypeStruct((TOK, 2 * D), BF),
        ),
        in_specs=[
            pl.BlockSpec(memory_space=pltpu.SMEM),
            anywhere,
            anywhere,
            vmem,
            anywhere,
            anywhere,
            vmem,
            vmem,
            vmem,
            vmem,
        ],
        out_specs=(vmem, anywhere),
        scratch_shapes=[
            pltpu.VMEM((D, TOK), BF),
            pltpu.VMEM((D, 3 * D), BF),
            pltpu.VMEM((D, TEXT), BF),
            pltpu.VMEM((2, TOK, 2 * D), BF),
            pltpu.VMEM((TOK, 2 * D), BF),
            pltpu.VMEM((TOK, 3 * D + 64), F32),
            pltpu.VMEM((TOK, 2 * D), BF),
            pltpu.VMEM((2, BLK, 2, TOK, 128), BF),
            pltpu.VMEM((2, BLK, 2, TOK, 128), BF),
            pltpu.VMEM((HEADS, HD, 128), BF),
            pltpu.VMEM((BLK, HD, 128), BF),
            pltpu.VMEM((SPARE, HD, 128), BF),
            pltpu.VMEM((ROWS + SPARE_ROWS, 128), BF),
            pltpu.VMEM((ROWS + SPARE_ROWS, 128), F32),
            pltpu.VMEM((TEXT_COLS, TEXT), F32),
            pltpu.VMEM((2, 128, TEXT), F32),
            pltpu.VMEM((2, TEXT, 128), BF),
            pltpu.VMEM((24, 128), F32),
            pltpu.VMEM((BLK + SPARE, HD, 128), BF),
            pltpu.VMEM((HEADS, HD, 128), BF),
            pltpu.VMEM((D, TOK), BF),
            dma((3,)),
            dma((D // W_ROWS,)),
            dma((2,)),
            dma((2, BLK)),
            dma,
            dma,
            dma((3,)),
            dma((SPARE,)),
            dma((TEXT_COLS // 8,)),
            dma((4, 6)),
            dma((2,)),
            dma,
            dma((SPARE,)),
            dma,
            dma,
            dma,
            dma,
        ],
        compiler_params=pltpu.CompilerParams(
            collective_id=0, has_side_effects=True, vmem_limit_bytes=56 * 1024 * 1024
        ),
    )(
        layer_patch_index,
        jnp.swapaxes(states[0], 0, 1),
        image_weight[0],
        jnp.swapaxes(text_weight[0], 0, 1),
        jnp.swapaxes(text_states[0], 0, 1),
        stale_cache[0],
        modulate,
        query_gain,
        key_gain,
        text_gain,
    )
    return (jnp.swapaxes(next_states, 0, 1)[None], fresh[None])


def solution(mesh):
    in_specs = (
        P("section", "blk", None),
        P("section", None, None),
        P("section", None, "blk"),
        P("section", None, None),
        P("section", None, "blk", None),
        P(None, "section", None, None),
        P("section", None),
        P("section", None),
        P("section", None),
        P("section"),
        P("section"),
    )
    out_specs = (P("section", "blk", None), P("section", "blk", None))
    return jax.shard_map(
        functools.partial(body, mesh.shape["section"]),
        mesh=mesh,
        in_specs=in_specs,
        out_specs=out_specs,
        check_vma=False,
    )
```

time: 244 us -> 118 us (0.48)
  waiting for transfers between devices: 141 us -> 0 us
  Pallas kernels: 0 us -> 111 us
  matrix products: 46.7 us -> 0 us
  local copies, waits for them, and re-layouts: 28 us -> 4.29 us
  between operations: 15.7 us -> 2.03 us
  other arithmetic: 9.81 us -> 0 us
  starting transfers between devices: 2.56 us -> 0 us
    all_gather x2 -> x0, waiting for transfers between devices: 133 us -> none  [the longest x1 116 us: body(): lax.all_gather(merged, 'blk', axis=0, tiled=True)]
    pallas_call x0 -> x1, Pallas kernels: none -> 111 us  [body(): pl.pallas_call(functools.partial(kernel, sections), out_shape=(jax.ShapeD...]
    dot_general x6 -> x0, matrix products: 46.7 us -> none  [the longest x2 18.9 us: partial_sums(): jnp.einsum('ckq,qcw->kcw', elementwise_powers.astype(jnp.bfloat16), value...]
    slice x4 -> x0, local copies, waits for them, and re-layouts: 15.6 us -> none  [the longest x1 15.6 us: partial_sums(): keys_block[:, :attn_width].reshape(key_rows, attention_channels, size_head)]
    ppermute x1 -> x0, waiting for transfers between devices: 7.96 us -> none  [passed_along(): return lax.ppermute(value, axis, pairs)]
    broadcast_in_dim x2 -> x0, local copies, waits for them, and re-layouts: 6.51 us -> none  [body(): jnp.where(slot_mask[:, None, None], fresh[None], stale_cache[0])]
    reduce_sum x8 -> x0, other arithmetic: 4.43 us -> none  [the longest x2 1.43 us: layer_norm(): center = values - jnp.mean(values, axis=-1, keepdims=True)]
    squeeze x1 -> x0, local copies, waits for them, and re-layouts: 2.63 us -> none  [body(): stale_cache[0]]
  transfers between devices with their start and end apart: 3 -> 0, of which waited for: 3 -> 0; matrix products, arithmetic and copies ran while one was open for 11% -> 0% of each run, Pallas kernels for 0% -> 0%
where the time goes in v1:
time: 118 us
  Pallas kernels  111 us (94%)
  local copies, waits for them, and re-layouts  4.29 us (4%)
  between operations  2.03 us (2%)
    pallas_call x1, Pallas kernels, body(): pl.pallas_call(functools.partial(kernel, sections), out_shape=(jax.ShapeD...  111 us
    unnamed x5, local copies, waits for them, and re-layouts  4.28 us

profile of v1, /device:TPU:1, one launch (start us, length us, event | category | flops | bytes accessed | tf_op | source)
XLA Modules:
  0.0 117.5 jit_solution(4449459328102937700)
XLA Ops:
  0.6 0.0 copy-start
  2.0 0.0 copy-done
  2.0 0.6 copy.15
  2.7 111.2 %shard_map.122 = (bf16[1216,128]{1,0:T(8,128)(2,1)}, bf16[128,2432]{1,0:T(8,128)(2,1)}) custom-call(s32[1]{0:T(128)S(6)} %copy.19.patch_ref, bf16[1216,128]{1,0:T(8,128)(2,1)} %bitcast.27, bf16[1216,3648]{1,0:T(8,128)(2,1)} %bitcast.22, bf16[152,1216]{1,0:T(8,128)(2,1)} %bitcast.26, bf16[1216,256]{1,0:T(8,128)(2,1)} %bitcast.24, ...), custom_call_target="tpu_custom_call" | custom-call | tf_op jit(solution)/shard_map/pallas_call | solution.py:543
  113.9 1.7 %copy.20 = bf16[1,128,1216]{1,2,0:T(8,128)(2,1)} copy(bf16[1,128,1216]{1,2,0:T(8,128)(2,1)} %bitcast.28) | data formatting | bytes 622592
  115.6 1.9 %copy.21 = bf16[1,128,2432]{2,1,0:T(8,128)(2,1)} copy(bf16[1,128,2432]{2,1,0:T(8,128)(2,1)} %bitcast.25) | data formatting | bytes 1245184
  (1 shorter events, 0.0 us)
Async XLA Ops:
  0.6 1.4 %copy-start = (f32[28,1,5,1216]{3,1,2,0:T(1,128)S(1)}, f32[28,1,5,1216]{3,1,2,0:T(1,128)}, u32[]{:S(2)}) copy-start(f32[28,1,5,1216]{3,1,2,0:T(1,128)} %param.16) | copy-start | bytes 2042884

commit v2 on v1

--- a/solution.py
+++ b/solution.py
@@ -23,7 +23,7 @@
 SPARE_ROWS = SPARE * TOK
 W_ROWS = 304
 SPARE_GROUPS = ((0, 6, 3), (6, 6, 3), (12, 4, 4))
-QT = 256
+QT = 512
 
 
 def low_half(rows):
@@ -90,7 +90,6 @@
     acc,
     text_send,
     text_recv,
-    text_kv,
     gate_v,
     out_send,
     out_recv,
@@ -157,7 +156,7 @@
             to = lax.rem(me + step, BLK)
             pltpu.make_async_remote_copy(
                 src_ref=kv_send.at[kind, to],
-                dst_ref=kv_recv.at[kind, me],
+                dst_ref=kv_recv.at[kind, :, me],
                 send_sem=kv_ssem.at[kind],
                 recv_sem=kv_rsem.at[kind, me],
                 device_id=(sec, to),
@@ -165,7 +164,7 @@
             ).start()
 
         pltpu.make_async_copy(
-            kv_send.at[kind, me], kv_recv.at[kind, me], kv_rsem.at[kind, me]
+            kv_send.at[kind, me], kv_recv.at[kind, :, me], kv_rsem.at[kind, me]
         ).start()
 
     load_stale.wait()
@@ -403,10 +402,11 @@
             pltpu.make_async_copy(q_spare.at[slot], q_spare.at[slot], spare_rsem.at[slot]).wait()
             spread_queries(q_spare[slot], ROWS + slot * TOK)
 
-    low256 = low_half(256)
-
-    def attend(entries, first, rows):
-        values = jnp.where(low256, jnp.ones((256, 128), F32), entries.astype(F32)).astype(BF)
+    def attend(kind, which, first, rows, sources):
+        entries = kv_recv[kind, which, 0:sources].reshape(sources * TOK, 128)
+        values = jnp.where(
+            low_half(sources * TOK), jnp.ones(entries.shape, F32), entries.astype(F32)
+        ).astype(BF)
 
         @pl.loop(0, rows // QT)
         def _(step):
@@ -415,27 +415,25 @@
                 q_all[at], entries, (((1,), (1,)), ((), ())), preferred_element_type=F32
             )
             powers = jnp.exp(scores).astype(BF)
-            acc[at] += jnp.dot(powers, values, preferred_element_type=F32)
-
-    acc[...] = jnp.zeros_like(acc)
-
-    def attend_patch(kind):
-        @pl.loop(0, BLK // 2)
-        def _(step):
-            pair = lax.rem(me // 2 + BLK // 2 - step, BLK // 2)
-            for core in range(2):
-                one_source = kv_recv.at[kind, 2 * pair + core]
-                pltpu.make_async_copy(
-                    one_source, one_source, kv_rsem.at[kind, 2 * pair + core]
-                ).wait()
-            for which, first, rows in ((0, 0, ROWS), (1, ROWS, SPARE_ROWS)):
-                entries = kv_recv[kind, pl.ds(2 * pair, 2), which].reshape(256, 128)
-                attend(entries, first, rows)
-
-    attend_patch(0)
-
+            sums = jnp.dot(powers, values, preferred_element_type=F32)
+            if kind == 0:
+                acc[at] = sums
+            else:
+                acc[at] += sums
+
+    def wait_entries(kind):
+        @pl.loop(0, BLK)
+        def _(source):
+            block = kv_recv.at[kind, :, source]
+            pltpu.make_async_copy(block, block, kv_rsem.at[kind, source]).wait()
+
+    wait_entries(0)
+    for which, first, rows in ((0, 0, ROWS), (1, ROWS, SPARE_ROWS)):
+        attend(0, which, first, rows, BLK)
+
+    low256 = low_half(TEXT)
     text_gain = jnp.concatenate([text_gain_ref[...], jnp.ones((1, HD), F32)], axis=1)
-    for which, first, rows in ((0, 0, ROWS), (1, ROWS, SPARE_ROWS)):
+    for which in range(2):
         pltpu.make_async_copy(
             text_recv.at[which], text_recv.at[which], text_rsem.at[which]
         ).wait()
@@ -443,10 +441,12 @@
         square = jnp.where(low256, value * value, 0.0)
         mean = jnp.sum(square, axis=1, keepdims=True) * (1.0 / HD)
         scaled = value * lax.rsqrt(mean + 1e-06) * text_gain
-        text_kv[which] = jnp.where(low256, scaled, value).astype(BF)
-        attend(text_kv[which], first, rows)
-
-    attend_patch(1)
+        text_entries = jnp.where(low256, scaled, value).astype(BF)
+        kv_recv[1, which, BLK : BLK + 2] = text_entries.reshape(2, TOK, 128)
+
+    wait_entries(1)
+    for which, first, rows in ((0, 0, ROWS), (1, ROWS, SPARE_ROWS)):
+        attend(1, which, first, rows, BLK + 2)
 
     def result_of(row, head):
         value = acc[pl.ds(row, TOK)] * gate_v[pl.ds(head, 1), :]
@@ -568,7 +568,7 @@
             pltpu.VMEM((TOK, 3 * D + 64), F32),
             pltpu.VMEM((TOK, 2 * D), BF),
             pltpu.VMEM((2, BLK, 2, TOK, 128), BF),
-            pltpu.VMEM((2, BLK, 2, TOK, 128), BF),
+            pltpu.VMEM((2, 2, BLK + 2, TOK, 128), BF),
             pltpu.VMEM((HEADS, HD, 128), BF),
             pltpu.VMEM((BLK, HD, 128), BF),
             pltpu.VMEM((SPARE, HD, 128), BF),
@@ -576,7 +576,6 @@
             pltpu.VMEM((ROWS + SPARE_ROWS, 128), F32),
             pltpu.VMEM((TEXT_COLS, TEXT), F32),
             pltpu.VMEM((2, 128, TEXT), F32),
-            pltpu.VMEM((2, TEXT, 128), BF),
             pltpu.VMEM((24, 128), F32),
             pltpu.VMEM((BLK + SPARE, HD, 128), BF),
             pltpu.VMEM((HEADS, HD, 128), BF),

time: 118 us -> 81 us (0.69)
  Pallas kernels: 111 us -> 74.5 us
    pallas_call x1, Pallas kernels: 111 us -> 74.5 us  [body(): pl.pallas_call(functools.partial(kernel, sections), out_shape=(jax.ShapeD...]
where the time goes in v2:
time: 81 us; the launch traced here: 80.8 us
  Pallas kernels  74.5 us (92%)
  local copies, waits for them, and re-layouts  4.29 us (5%)
  between operations  2.03 us (3%)
    pallas_call x1, Pallas kernels, body(): pl.pallas_call(functools.partial(kernel, sections), out_shape=(jax.ShapeD...  74.5 us
    unnamed x5, local copies, waits for them, and re-layouts  4.28 us

profile of v2, /device:TPU:1, one launch (start us, length us, event | category | flops | bytes accessed | tf_op | source)
XLA Modules:
  0.0 80.8 jit_solution(4943892740417323713)
XLA Ops:
  0.6 0.0 copy-start
  2.0 0.0 copy-done
  2.0 0.6 copy.15
  2.7 74.5 %shard_map.122 = (bf16[1216,128]{1,0:T(8,128)(2,1)}, bf16[128,2432]{1,0:T(8,128)(2,1)}) custom-call(s32[1]{0:T(128)S(6)} %copy.19.patch_ref, bf16[1216,128]{1,0:T(8,128)(2,1)} %bitcast.27, bf16[1216,3648]{1,0:T(8,128)(2,1)} %bitcast.22, bf16[152,1216]{1,0:T(8,128)(2,1)} %bitcast.26, bf16[1216,256]{1,0:T(8,128)(2,1)} %bitcast.24, ...), custom_call_target="tpu_custom_call" | custom-call | tf_op jit(solution)/shard_map/pallas_call | solution.py:543
  77.1 1.7 %copy.20 = bf16[1,128,1216]{1,2,0:T(8,128)(2,1)} copy(bf16[1,128,1216]{1,2,0:T(8,128)(2,1)} %bitcast.28) | data formatting | bytes 622592
  78.8 1.9 %copy.21 = bf16[1,128,2432]{2,1,0:T(8,128)(2,1)} copy(bf16[1,128,2432]{2,1,0:T(8,128)(2,1)} %bitcast.25) | data formatting | bytes 1245184
  (1 shorter events, 0.0 us)
Async XLA Ops:
  0.6 1.4 %copy-start = (f32[28,1,5,1216]{3,1,2,0:T(1,128)S(1)}, f32[28,1,5,1216]{3,1,2,0:T(1,128)}, u32[]{:S(2)}) copy-start(f32[28,1,5,1216]{3,1,2,0:T(1,128)} %param.16) | copy-start | bytes 2042884

commit v3 on v2

v3 whole, which is shorter than its diff:
```python
import functools

import jax
import jax.numpy as jnp
from jax import lax
from jax.experimental import pallas as pl
from jax.experimental.pallas import tpu as pltpu
from jax.sharding import PartitionSpec as P

MESH = pl.DeviceIdType.MESH
BF = jnp.bfloat16
F32 = jnp.float32

D = 1216
HEADS = 19
HD = 64
TOK = 128
TEXT = 256
BLK = 16
TEXT_COLS = 152
SPARE = 4
ROWS = BLK * TOK
SPARE_ROWS = SPARE * TOK
W_ROWS = 304
SPARE_DEVICES = 4
SPARE_HEADS = 3
QT = 512


def low_half(rows):
    return lax.broadcasted_iota(jnp.int32, (rows, 128), 1) < HD


def swap_halves(value):
    return pltpu.roll(value, HD, axis=1)


def layer_norm(values):
    center = values - jnp.mean(values, axis=-1, keepdims=True)
    return center * lax.rsqrt(jnp.mean(center * center, axis=-1, keepdims=True) + 1e-06)


def pack_heads(source, mains, spares):
    low = low_half(TOK)

    def tile(index):
        return source[:, 128 * index : 128 * index + 128].astype(F32)

    for head in range(HEADS):
        half = head // 2
        if head % 2 == 0:
            packed = jnp.where(low, tile(half), tile(9 + half))
        else:
            packed = swap_halves(jnp.where(low, tile(10 + half), tile(half)))
        if head < BLK:
            mains[head] = packed.astype(BF)
        else:
            spares[head - BLK] = packed.astype(BF)


def kernel(
    sections,
    patch_ref,
    step_ref,
    states_hbm,
    weight_hbm,
    text_weight_ref,
    text_hbm,
    stale_hbm,
    mod_hbm,
    query_gain_ref,
    key_gain_ref,
    text_gain_ref,
    out_hbm,
    fresh_hbm,
    states_v,
    weight_v,
    text_v,
    stale_v,
    mod_v,
    entries_v,
    proj_v,
    fresh_v,
    main_send,
    main_recv,
    spare_send,
    spare_recv,
    q_send,
    q_recv,
    q_spare,
    q_all,
    state_recv,
    state_spare,
    acc,
    text_send,
    text_recv,
    gate_v,
    out_send,
    load_sem,
    weight_sem,
    main_ssem,
    main_rsem,
    spare_ssem,
    spare_rsem,
    pass_ssem,
    pass_rsem,
    q_ssem,
    q_rsem,
    q_ssem2,
    q_rsem2,
    state_ssem,
    state_rsem,
    state_ssem2,
    state_rsem2,
    text_ssem,
    text_ssem2,
    text_rsem,
    out_ssem,
    out_ssem2,
    out_rsem,
    fresh_sem,
):
    sec = lax.axis_index("section")
    me = lax.axis_index("blk")
    after = lax.rem(sec + 1, sections)
    before = lax.rem(sec + sections - 1, sections)

    load_stale = pltpu.make_async_copy(stale_hbm, stale_v, load_sem.at[0])
    load_states = pltpu.make_async_copy(states_hbm, states_v, load_sem.at[1])
    load_text = pltpu.make_async_copy(text_hbm, text_v, load_sem.at[2])
    load_mod = pltpu.make_async_copy(mod_hbm, mod_v, load_sem.at[3])
    load_stale.start()
    load_states.start()
    load_mod.start()
    loads = []
    for part in range(D // W_ROWS):
        rows = pl.ds(part * W_ROWS, W_ROWS)
        loads.append(
            pltpu.make_async_copy(weight_hbm.at[rows], weight_v.at[rows], weight_sem.at[part])
        )
        loads[-1].start()
    load_text.start()

    barrier = pltpu.get_barrier_semaphore()

    @pl.loop(1, BLK)
    def _(step):
        pl.semaphore_signal(
            barrier, inc=1, device_id=(sec, lax.rem(me + step, BLK)), device_id_type=MESH
        )

    @pl.loop(0, BLK)
    def _(step):
        pl.semaphore_signal(
            barrier, inc=1, device_id=(before, lax.rem(me + step, BLK)), device_id_type=MESH
        )

    core = lax.rem(me, 2)
    chip = me // 2
    sibling = me + 1 - 2 * core
    spare_index = me // SPARE_DEVICES
    has_spare = spare_index < SPARE_HEADS
    first_block = SPARE * lax.rem(me, SPARE_DEVICES)
    SPARE_CHIPS = SPARE_HEADS * SPARE_DEVICES // 2

    def remote(source, target, send, recv, to, section=None):
        return pltpu.make_async_remote_copy(
            src_ref=source,
            dst_ref=target,
            send_sem=send,
            recv_sem=recv,
            device_id=(sec if section is None else section, to),
            device_id_type=MESH,
        )

    def arrived(ref, sem):
        pltpu.make_async_copy(ref, ref, sem).wait()

    def send_main(kind):
        @pl.loop(1, BLK)
        def _(step):
            to = lax.rem(me + step, BLK)
            remote(
                main_send.at[kind, to],
                main_recv.at[kind, me],
                main_ssem.at[kind],
                main_rsem.at[kind],
                to,
            ).start()

        pltpu.make_async_copy(
            main_send.at[kind, me], main_recv.at[kind, me], main_rsem.at[kind]
        ).start()

    def spare_copy(kind, to_chip):
        return remote(
            spare_send.at[kind, 2 * to_chip // SPARE_DEVICES],
            spare_recv.at[kind, 8 * core + chip],
            spare_ssem.at[kind, to_chip],
            spare_rsem.at[kind],
            2 * to_chip + core,
        )

    def send_spare(kind):
        @pl.loop(0, BLK // 2)
        def _(step):
            to_chip = lax.rem(chip + step, BLK // 2)

            @pl.when(jnp.logical_and(to_chip != chip, to_chip < SPARE_CHIPS))
            def _():
                spare_copy(kind, to_chip).start()

        @pl.when(has_spare)
        def _():
            pltpu.make_async_copy(
                spare_send.at[kind, spare_index],
                spare_recv.at[kind, 8 * core + chip],
                spare_rsem.at[kind],
            ).start()

    def pass_copy(kind):
        block = spare_recv.at[kind, pl.ds(8 * core, 8)]
        return remote(block, block, pass_ssem.at[kind], pass_rsem.at[kind], sibling)

    def pass_spare(kind):
        @pl.when(has_spare)
        def _():
            arrived(spare_recv.at[kind, pl.ds(8 * core, 8)], spare_rsem.at[kind])
            pass_copy(kind).start()

    load_stale.wait()
    first_worked = patch_ref[0] == 0
    for index in range(HEADS):
        cols = slice(128 * index, 128 * index + 128)
        entries_v[:, cols] = jnp.where(first_worked, stale_v[1, :, cols], stale_v[0, :, cols])
    pack_heads(entries_v, main_send.at[0], spare_send.at[0])
    pl.semaphore_wait(barrier, 2 * BLK - 1)
    send_main(0)

    load_states.wait()
    load_mod.wait()
    row = step_ref[0]
    normed = (
        layer_norm(states_v[...].astype(F32).T) * (1.0 + mod_v[row, 1]) + mod_v[row, 0]
    ).astype(BF)
    for load in loads:
        load.wait()

    block_ones = (
        (lax.broadcasted_iota(jnp.int32, (128, 128), 0) < HD)
        == (lax.broadcasted_iota(jnp.int32, (128, 128), 1) < HD)
    ).astype(BF)
    query_gain = query_gain_ref[...]
    key_gain = key_gain_ref[...]

    def project(first, last):
        proj_v[:, first:last] = jnp.dot(
            normed, weight_v[:, first:last], preferred_element_type=F32
        )

    def normed_tile(index):
        value = proj_v[:, 128 * index : 128 * index + 128]
        square = value * value
        high = square.astype(BF)
        low = (square - high.astype(F32)).astype(BF)
        mean = (
            jnp.dot(high, block_ones, preferred_element_type=F32)
            + jnp.dot(low, block_ones, preferred_element_type=F32)
        ) * (1.0 / HD)
        gain = jnp.concatenate(
            [
                query_gain if index < 10 else key_gain,
                query_gain if index < 9 else key_gain,
            ],
            axis=1,
        )
        return value * lax.rsqrt(mean + 1e-06) * gain

    low64 = low_half(HD)
    project(0, 1280)
    for index in range(10):
        value = normed_tile(index)
        if index == 9:
            proj_v[:, 128 * index : 128 * index + 128] = value
        top, bottom = value[:HD], value[HD:]
        even = jnp.where(low64, top, swap_halves(bottom))
        q_send[2 * index] = (even.astype(BF).astype(F32) * 0.125).astype(BF)
        if index < 9:
            odd = jnp.where(low64, swap_halves(top), bottom)
            q_send[2 * index + 1] = (odd.astype(BF).astype(F32) * 0.125).astype(BF)

    @pl.loop(1, BLK)
    def _(step):
        to = lax.rem(me + step, BLK)
        remote(q_send.at[to], q_recv.at[me], q_ssem, q_rsem, to).start()

    pltpu.make_async_copy(q_send.at[me], q_recv.at[me], q_rsem).start()

    slot_there = lax.rem(me, SPARE)

    def spare_target(index):
        return SPARE_DEVICES * index + me // SPARE

    def query_copy(index):
        return remote(
            q_send.at[BLK + index],
            q_spare.at[slot_there],
            q_ssem2.at[index],
            q_rsem2.at[slot_there],
            spare_target(index),
        )

    def state_rows(head):
        return states_v.at[pl.ds(pl.multiple_of(HD * head, HD), HD)]

    def state_copy(index):
        return remote(
            state_rows(BLK + index),
            state_spare.at[slot_there],
            state_ssem2.at[index],
            state_rsem2.at[slot_there],
            spare_target(index),
        )

    for index in range(SPARE_HEADS):

        @pl.when(spare_target(index) != me)
        def _():
            query_copy(index).start()

        @pl.when(spare_target(index) == me)
        def _():
            pltpu.make_async_copy(
                q_send.at[BLK + index], q_spare.at[slot_there], q_rsem2.at[slot_there]
            ).start()

    project(1280, 2432)
    project(2432, 3648)
    low = low_half(TOK)

    def swapped_tile(index):
        if index == 9 or index >= 19:
            return swap_halves(proj_v[:, 128 * index : 128 * index + 128])
        return swap_halves(normed_tile(index))

    left = swapped_tile(9)
    for index in range(HEADS):
        right = swapped_tile(10 + index)
        fresh_v[:, 128 * index : 128 * index + 128] = jnp.where(low, left, right).astype(BF)
        left = right
    fresh_copy = pltpu.make_async_copy(fresh_v, fresh_hbm, fresh_sem)
    fresh_copy.start()
    pack_heads(fresh_v, main_send.at[1], spare_send.at[1])
    send_main(1)

    @pl.loop(1, BLK)
    def _(step):
        to = lax.rem(me + step, BLK)
        remote(state_rows(to), state_recv.at[me], state_ssem, state_rsem, to).start()

    pltpu.make_async_copy(state_rows(me), state_recv.at[me], state_rsem).start()
    for index in range(SPARE_HEADS):

        @pl.when(spare_target(index) != me)
        def _():
            state_copy(index).start()

        @pl.when(spare_target(index) == me)
        def _():
            pltpu.make_async_copy(
                state_rows(BLK + index), state_spare.at[slot_there], state_rsem2.at[slot_there]
            ).start()

    send_spare(0)
    send_spare(1)

    load_text.wait()
    text_normed = (
        layer_norm(text_v[...].astype(F32).T) * (1.0 + mod_v[row, 4]) + mod_v[row, 3]
    ).astype(BF)
    text_send[...] = (
        lax.dot_general(
            text_weight_ref[...],
            text_normed,
            (((1,), (1,)), ((), ())),
            preferred_element_type=F32,
        )
        .astype(BF)
        .astype(F32)
    )

    def text_main(step):
        unit = TEXT_COLS // 8 * me + step
        second = unit // TEXT_COLS
        head = (unit - TEXT_COLS * second) // 8
        to_row = pl.multiple_of(HD * second + 8 * lax.rem(unit, 8), 8)
        source = text_send.at[pl.ds(pl.multiple_of(8 * step, 8), 8)]
        target = text_recv.at[0, pl.ds(to_row, 8)]
        return (
            head,
            lambda: remote(source, target, text_ssem.at[step], text_rsem.at[0], head),
            lambda: pltpu.make_async_copy(source, target, text_rsem.at[0]),
        )

    @pl.loop(0, TEXT_COLS // 8)
    def _(step):
        head, away, local = text_main(step)

        @pl.when(jnp.logical_and(head < BLK, head != me))
        def _():
            away().start()

        @pl.when(head == me)
        def _():
            local().start()

    pieces = ((6, 112, 40, 0, 0), (7, 0, 24, 0, 40), (7, 24, 64, 1, 0), (7, 88, 64, 2, 0))
    second_half = me // 8

    def text_spare(number, step):
        _, row, rows, index, to_row = pieces[number]
        to = SPARE_DEVICES * index + step
        source = text_send.at[pl.ds(row, rows)]
        target = text_recv.at[1, pl.ds(pl.multiple_of(HD * second_half + to_row, 8), rows)]
        return (
            to,
            lambda: remote(source, target, text_ssem2.at[number, step], text_rsem.at[1], to),
            lambda: pltpu.make_async_copy(source, target, text_rsem.at[1]),
        )

    for number in range(4):

        @pl.when(lax.rem(me, 8) == pieces[number][0])
        def _():
            @pl.loop(0, SPARE_DEVICES)
            def _(step):
                to, away, local = text_spare(number, step)

                @pl.when(to != me)
                def _():
                    away().start()

                @pl.when(to == me)
                def _():
                    local().start()

    one = jnp.ones((1, 128), F32)
    low1 = low_half(1)
    gate_pad = jnp.concatenate([mod_v[row, 2], jnp.zeros((1, 64), F32)], axis=1)
    for head in range(HEADS):
        gate = gate_pad[:, 128 * (head // 2) : 128 * (head // 2) + 128]
        if head % 2 == 0:
            gate = swap_halves(jnp.broadcast_to(gate, (8, 128)))[0:1]
        gate_v[head : head + 1, :] = jnp.where(low1, one, gate)

    arrived(q_recv, q_rsem)

    def spread_queries(packed, row):
        value = packed.astype(F32)
        zero = jnp.zeros_like(value)
        q_all[pl.ds(row, HD)] = jnp.where(low64, value, zero).astype(BF)
        q_all[pl.ds(row + HD, HD)] = jnp.where(low64, swap_halves(value), zero).astype(BF)

    @pl.loop(0, BLK)
    def _(step):
        spread_queries(q_recv[step], pl.multiple_of(step * TOK, TOK))

    @pl.when(has_spare)
    def _():
        for slot in range(SPARE):
            arrived(q_spare.at[slot], q_rsem2.at[slot])
            spread_queries(q_spare[slot], ROWS + slot * TOK)

    def with_ones(entries):
        return jnp.where(
            low_half(entries.shape[0]), jnp.ones(entries.shape, F32), entries.astype(F32)
        ).astype(BF)

    def attend(rows, entries, values):
        scores = lax.dot_general(
            q_all[rows], entries, (((1,), (1,)), ((), ())), preferred_element_type=F32
        )
        powers = jnp.exp(scores).astype(BF)
        return jnp.dot(powers, values, preferred_element_type=F32)

    def query_rows(step):
        return pl.ds(pl.multiple_of(step * QT, QT), QT)

    arrived(main_recv.at[0, pl.ds(0, BLK)], main_rsem.at[0])
    stale_entries = main_recv[0, 0:BLK].reshape(BLK * TOK, 128)
    stale_values = with_ones(stale_entries)

    @pl.loop(0, ROWS // QT)
    def _(step):
        acc[query_rows(step)] = attend(query_rows(step), stale_entries, stale_values)

    low256 = low_half(TEXT)
    text_gain = jnp.concatenate([text_gain_ref[...], jnp.ones((1, HD), F32)], axis=1)

    def text_entries(which):
        arrived(text_recv.at[which], text_rsem.at[which])
        value = text_recv[which].T
        square = jnp.where(low256, value * value, 0.0)
        mean = jnp.sum(square, axis=1, keepdims=True) * (1.0 / HD)
        scaled = value * lax.rsqrt(mean + 1e-06) * text_gain
        return jnp.where(low256, scaled, value).astype(BF).reshape(2, TOK, 128)

    main_recv[1, BLK : BLK + 2] = text_entries(0)
    arrived(main_recv.at[1, pl.ds(0, BLK)], main_rsem.at[1])
    fresh_entries = main_recv[1].reshape((BLK + 2) * TOK, 128)
    fresh_values = with_ones(fresh_entries)

    def result_of(row, head, states):
        value = acc[pl.ds(row, TOK)] * gate_v[pl.ds(head, 1), :]
        turned = value.T
        return (states.astype(F32) + turned[HD:] / turned[:HD]).astype(BF)

    def result_copy(slot, head, block, sem):
        target = out_hbm.at[pl.ds(pl.multiple_of(HD * head, HD), HD)]
        return remote(out_send.at[slot], target, sem, out_rsem, block, after)

    def finish(step):
        acc[query_rows(step)] += attend(query_rows(step), fresh_entries, fresh_values)
        for part in range(QT // TOK):
            block = step * (QT // TOK) + part
            out_send[block] = result_of(
                pl.multiple_of(block * TOK, TOK), me, state_recv[block]
            )
            result_copy(block, me, block, out_ssem).start()

    arrived(state_recv, state_rsem)
    pass_spare(0)
    finish(0)
    pass_spare(1)
    pl.loop(1, ROWS // QT)(finish)

    @pl.when(has_spare)
    def _():
        spare_recv[1, BLK : BLK + 2] = text_entries(1)
        for kind in range(2):
            arrived(spare_recv.at[kind, pl.ds(8 * (1 - core), 8)], pass_rsem.at[kind])
            pass_copy(kind).wait_send()
        rows = pl.ds(ROWS, SPARE_ROWS)
        total = jnp.zeros((SPARE_ROWS, 128), F32)
        for kind, tiles in ((0, BLK), (1, BLK + 2)):
            entries = spare_recv[kind, 0:tiles].reshape(tiles * TOK, 128)
            total = total + attend(rows, entries, with_ones(entries))
        acc[rows] = total
        for slot in range(SPARE):
            arrived(state_spare.at[slot], state_rsem2.at[slot])
            out_send[BLK + slot] = result_of(
                ROWS + slot * TOK, BLK + spare_index, state_spare[slot]
            )
            result_copy(
                BLK + slot, BLK + spare_index, first_block + slot, out_ssem2.at[slot]
            ).start()

    arrived(out_hbm, out_rsem)

    fresh_copy.wait()
    for kind in range(2):
        arrived(main_send.at[kind, pl.ds(0, BLK - 1)], main_ssem.at[kind])

        @pl.loop(0, SPARE_CHIPS)
        def _(to_chip):
            @pl.when(to_chip != chip)
            def _():
                spare_copy(kind, to_chip).wait_send()

    arrived(q_send.at[pl.ds(0, BLK - 1)], q_ssem)
    arrived(state_recv.at[pl.ds(0, BLK - 1)], state_ssem)
    for index in range(SPARE_HEADS):

        @pl.when(spare_target(index) != me)
        def _():
            query_copy(index).wait_send()
            state_copy(index).wait_send()

    @pl.loop(0, TEXT_COLS // 8)
    def _(step):
        head, away, _ = text_main(step)

        @pl.when(jnp.logical_and(head < BLK, head != me))
        def _():
            away().wait_send()

    for number in range(4):

        @pl.when(lax.rem(me, 8) == pieces[number][0])
        def _():
            @pl.loop(0, SPARE_DEVICES)
            def _(step):
                to, away, _ = text_spare(number, step)

                @pl.when(to != me)
                def _():
                    away().wait_send()

    arrived(out_send.at[pl.ds(0, BLK)], out_ssem)

    @pl.when(has_spare)
    def _():
        for slot in range(SPARE):
            result_copy(
                BLK + slot, BLK + spare_index, first_block + slot, out_ssem2.at[slot]
            ).wait_send()


def write_results(raw_states, raw_fresh, states_out, fresh_out, sems):
    copies = (
        pltpu.make_async_copy(raw_states, states_out, sems.at[0]),
        pltpu.make_async_copy(raw_fresh, fresh_out, sems.at[1]),
    )
    for copy in copies:
        copy.start()
    for copy in copies:
        copy.wait()


def body(
    sections,
    states,
    image_weight,
    text_weight,
    text_states,
    stale_cache,
    modulation,
    query_gain,
    key_gain,
    text_gain,
    timestep,
    layer_patch_index,
):
    vmem = pl.BlockSpec(memory_space=pltpu.VMEM)
    anywhere = pl.BlockSpec(memory_space=pl.ANY)
    dma = pltpu.SemaphoreType.DMA
    next_states, fresh = pl.pallas_call(
        functools.partial(kernel, sections),
        out_shape=(
            jax.ShapeDtypeStruct((D, TOK), BF),
            jax.ShapeDtypeStruct((TOK, 2 * D), BF),
        ),
        in_specs=[
            pl.BlockSpec(memory_space=pltpu.SMEM),
            pl.BlockSpec(memory_space=pltpu.SMEM),
            anywhere,
            anywhere,
            vmem,
            anywhere,
            anywhere,
            anywhere,
            vmem,
            vmem,
            vmem,
        ],
        out_specs=(anywhere, anywhere),
        scratch_shapes=[
            pltpu.VMEM((D, TOK), BF),
            pltpu.VMEM((D, 3 * D), BF),
            pltpu.VMEM((D, TEXT), BF),
            pltpu.VMEM((2, TOK, 2 * D), BF),
            pltpu.VMEM((modulation.shape[0], 5, 1, D), F32),
            pltpu.VMEM((TOK, 2 * D), BF),
            pltpu.VMEM((TOK, 3 * D + 64), F32),
            pltpu.VMEM((TOK, 2 * D), BF),
            pltpu.VMEM((2, BLK, TOK, 128), BF),
            pltpu.VMEM((2, BLK + 2, TOK, 128), BF),
            pltpu.VMEM((2, SPARE_HEADS, TOK, 128), BF),
            pltpu.VMEM((2, BLK + 2, TOK, 128), BF),
            pltpu.VMEM((HEADS, HD, 128), BF),
            pltpu.VMEM((BLK, HD, 128), BF),
            pltpu.VMEM((SPARE, HD, 128), BF),
            pltpu.VMEM((ROWS + SPARE_ROWS, 128), BF),
            pltpu.VMEM((BLK, HD, 128), BF),
            pltpu.VMEM((SPARE, HD, 128), BF),
            pltpu.VMEM((ROWS + SPARE_ROWS, 128), F32),
            pltpu.VMEM((TEXT_COLS, TEXT), F32),
            pltpu.VMEM((2, 128, TEXT), F32),
            pltpu.VMEM((24, 128), F32),
            pltpu.VMEM((BLK + SPARE, HD, 128), BF),
            dma((4,)),
            dma((D // W_ROWS,)),
            dma((2,)),
            dma((2,)),
            dma((2, BLK // 2)),
            dma((2,)),
            dma((2,)),
            dma((2,)),
            dma,
            dma,
            dma((SPARE_HEADS,)),
            dma((SPARE,)),
            dma,
            dma,
            dma((SPARE_HEADS,)),
            dma((SPARE,)),
            dma((TEXT_COLS // 8,)),
            dma((4, SPARE_DEVICES)),
            dma((2,)),
            dma,
            dma((SPARE,)),
            dma,
            dma,
        ],
        compiler_params=pltpu.CompilerParams(
            collective_id=0, has_side_effects=True, vmem_limit_bytes=56 * 1024 * 1024
        ),
    )(
        layer_patch_index,
        timestep,
        jnp.swapaxes(states[0], 0, 1),
        image_weight[0],
        jnp.swapaxes(text_weight[0], 0, 1),
        jnp.swapaxes(text_states[0], 0, 1),
        stale_cache[0],
        jnp.swapaxes(modulation, 1, 2),
        query_gain,
        key_gain,
        text_gain,
    )
    next_states, fresh = pl.pallas_call(
        write_results,
        out_shape=(
            jax.ShapeDtypeStruct((D, TOK), BF),
            jax.ShapeDtypeStruct((TOK, 2 * D), BF),
        ),
        in_specs=[anywhere, anywhere],
        out_specs=(anywhere, anywhere),
        scratch_shapes=[dma((2,))],
        compiler_params=pltpu.CompilerParams(vmem_limit_bytes=60 * 1024 * 1024),
    )(next_states, fresh)
    return (jnp.swapaxes(next_states, 0, 1)[None], fresh[None])


def solution(mesh):
    in_specs = (
        P("section", "blk", None),
        P("section", None, None),
        P("section", None, "blk"),
        P("section", None, None),
        P("section", None, "blk", None),
        P(None, "section", None, None),
        P("section", None),
        P("section", None),
        P("section", None),
        P("section"),
        P("section"),
    )
    out_specs = (P("section", "blk", None), P("section", "blk", None))
    return jax.shard_map(
        functools.partial(body, mesh.shape["section"]),
        mesh=mesh,
        in_specs=in_specs,
        out_specs=out_specs,
        check_vma=False,
    )
```

time: 81 us -> 93 us (1.15)
  Pallas kernels: 74.5 us -> 90.8 us
  local copies, waits for them, and re-layouts: 4.29 us -> 0 us
    pallas_call x0 -> x1, Pallas kernels: none -> 29.4 us  [body(): pl.pallas_call(write_results, out_shape=(jax.ShapeDtypeStruct((D, TOK), B...]
    pallas_call x1, Pallas kernels: 74.5 us -> 61.4 us  [body(): pl.pallas_call(functools.partial(kernel, sections), out_shape=(jax.ShapeD...]
    unnamed x5 -> x0, local copies, waits for them, and re-layouts: 4.28 us -> none
where the time goes in v3:
time: 93 us; the launch traced here: 92.9 us
  Pallas kernels  90.8 us (98%)
  between operations  2.09 us (2%)
    pallas_call x1, Pallas kernels, body(): pl.pallas_call(functools.partial(kernel, sections), out_shape=(jax.ShapeD...  61.4 us
    pallas_call x1, Pallas kernels, body(): pl.pallas_call(write_results, out_shape=(jax.ShapeDtypeStruct((D, TOK), B...  29.4 us

profile of v3, /device:TPU:1, one launch (start us, length us, event | category | flops | bytes accessed | tf_op | source)
XLA Modules:
  0.0 92.9 jit_solution(14312939313554509030)
XLA Ops:
  1.9 61.4 %shard_map.122 = (bf16[1216,128]{1,0:T(8,128)(2,1)}, bf16[128,2432]{1,0:T(8,128)(2,1)}) custom-call(s32[1]{0:T(128)S(6)} %copy.14.patch_ref, s32[1]{0:T(128)S(6)} %copy.13.step_ref, bf16[1216,128]{1,0:T(8,128)(2,1)} %bitcast.21, bf16[1216,3648]{1,0:T(8,128)(2,1)} %bitcast.16, bf16[152,1216]{1,0:T(8,128)(2,1)} %bitcast.20, bf16[1216,256]{1,0:T(8,128)(2,1)} %bitcast.19, ...), custom_call_target="tpu_custom_call" | custom-call | tf_op jit(solution)/shard_map/pallas_call | solution.py:637
  63.3 29.4 %shard_map.123 = (bf16[1216,128]{1,0:T(8,128)(2,1)}, bf16[128,2432]{1,0:T(8,128)(2,1)}) custom-call(bf16[1216,128]{1,0:T(8,128)(2,1)} %get-tuple-element.6.raw_states, bf16[128,2432]{1,0:T(8,128)(2,1)} %get-tuple-element.7.raw_fresh), custom_call_target="tpu_custom_call" | custom-call | tf_op jit(solution)/shard_map/pallas_call | solution.py:721

commit v4 on v3

--- a/solution.py
+++ b/solution.py
@@ -132,6 +132,7 @@
     load_stale.start()
     load_states.start()
     load_mod.start()
+    load_text.start()
     loads = []
     for part in range(D // W_ROWS):
         rows = pl.ds(part * W_ROWS, W_ROWS)
@@ -139,7 +140,6 @@
             pltpu.make_async_copy(weight_hbm.at[rows], weight_v.at[rows], weight_sem.at[part])
         )
         loads[-1].start()
-    load_text.start()
 
     barrier = pltpu.get_barrier_semaphore()
 
@@ -162,6 +162,15 @@
     has_spare = spare_index < SPARE_HEADS
     first_block = SPARE * lax.rem(me, SPARE_DEVICES)
     SPARE_CHIPS = SPARE_HEADS * SPARE_DEVICES // 2
+
+    def peer(step):
+        ring = step // 4
+        up = jnp.where(ring == 0, 2, jnp.where(ring == 1, 1, jnp.where(ring == 2, 3, 0)))
+        rest = lax.rem(step, 4)
+        to_x = lax.rem(me // 8 + 1 - rest // 2, 2)
+        to_y = lax.rem(chip + up, 4)
+        to_core = lax.rem(core + 1 - lax.rem(rest, 2), 2)
+        return 8 * to_x + 2 * to_y + to_core
 
     def remote(source, target, send, recv, to, section=None):
         return pltpu.make_async_remote_copy(
@@ -177,9 +186,9 @@
         pltpu.make_async_copy(ref, ref, sem).wait()
 
     def send_main(kind):
-        @pl.loop(1, BLK)
+        @pl.loop(0, BLK - 1)
         def _(step):
-            to = lax.rem(me + step, BLK)
+            to = peer(step)
             remote(
                 main_send.at[kind, to],
                 main_recv.at[kind, me],
@@ -204,7 +213,7 @@
     def send_spare(kind):
         @pl.loop(0, BLK // 2)
         def _(step):
-            to_chip = lax.rem(chip + step, BLK // 2)
+            to_chip = peer(2 * step) // 2
 
             @pl.when(jnp.logical_and(to_chip != chip, to_chip < SPARE_CHIPS))
             def _():
@@ -237,9 +246,103 @@
     pl.semaphore_wait(barrier, 2 * BLK - 1)
     send_main(0)
 
-    load_states.wait()
+    load_text.wait()
     load_mod.wait()
     row = step_ref[0]
+    text_normed = (
+        layer_norm(text_v[...].astype(F32).T) * (1.0 + mod_v[row, 4]) + mod_v[row, 3]
+    ).astype(BF)
+    text_part = lax.dot_general(
+        text_weight_ref[...],
+        text_normed,
+        (((1,), (1,)), ((), ())),
+        preferred_element_type=F32,
+    )
+    for unit in range(TEXT_COLS // 8):
+        eight = text_part[8 * unit : 8 * unit + 8]
+        text_send[unit] = jnp.concatenate([eight[:, :128], eight[:, 128:]], axis=0).astype(BF)
+
+    def text_main(step):
+        unit = TEXT_COLS // 8 * me + step
+        second = unit // TEXT_COLS
+        head = (unit - TEXT_COLS * second) // 8
+        source = text_send.at[step]
+        target = text_recv.at[0, 8 * second + lax.rem(unit, 8)]
+        return (
+            head,
+            lambda: remote(source, target, text_ssem.at[step], text_rsem.at[0], head),
+            lambda: pltpu.make_async_copy(source, target, text_rsem.at[0]),
+        )
+
+    @pl.loop(0, TEXT_COLS // 8)
+    def _(step):
+        head, away, local = text_main(step)
+
+        @pl.when(jnp.logical_and(head < BLK, head != me))
+        def _():
+            away().start()
+
+        @pl.when(head == me)
+        def _():
+            local().start()
+
+    pieces = ((6, 14, 5, 0, 0), (7, 0, 3, 0, 5), (7, 3, 8, 1, 0), (7, 11, 8, 2, 0))
+    second_half = me // 8
+
+    def text_spare(number, step):
+        _, row, rows, index, to_row = pieces[number]
+        to = SPARE_DEVICES * index + step
+        source = text_send.at[pl.ds(row, rows)]
+        target = text_recv.at[1, pl.ds(8 * second_half + to_row, rows)]
+        return (
+            to,
+            lambda: remote(source, target, text_ssem2.at[number, step], text_rsem.at[1], to),
+            lambda: pltpu.make_async_copy(source, target, text_rsem.at[1]),
+        )
+
+    for number in range(4):
+
+        @pl.when(lax.rem(me, 8) == pieces[number][0])
+        def _():
+            @pl.loop(0, SPARE_DEVICES)
+            def _(step):
+                to, away, local = text_spare(number, step)
+
+                @pl.when(to != me)
+                def _():
+                    away().start()
+
+                @pl.when(to == me)
+                def _():
+                    local().start()
+
+    slot_there = lax.rem(me, SPARE)
+
+    def spare_target(index):
+        return SPARE_DEVICES * index + me // SPARE
+
+    def query_copy(index):
+        return remote(
+            q_send.at[BLK + index],
+            q_spare.at[slot_there],
+            q_ssem2.at[index],
+            q_rsem2.at[slot_there],
+            spare_target(index),
+        )
+
+    def state_rows(head):
+        return states_v.at[pl.ds(pl.multiple_of(HD * head, HD), HD)]
+
+    def state_copy(index):
+        return remote(
+            state_rows(BLK + index),
+            state_spare.at[slot_there],
+            state_ssem2.at[index],
+            state_rsem2.at[slot_there],
+            spare_target(index),
+        )
+
+    load_states.wait()
     normed = (
         layer_norm(states_v[...].astype(F32).T) * (1.0 + mod_v[row, 1]) + mod_v[row, 0]
     ).astype(BF)
@@ -289,38 +392,12 @@
             odd = jnp.where(low64, swap_halves(top), bottom)
             q_send[2 * index + 1] = (odd.astype(BF).astype(F32) * 0.125).astype(BF)
 
-    @pl.loop(1, BLK)
+    @pl.loop(0, BLK - 1)
     def _(step):
-        to = lax.rem(me + step, BLK)
+        to = peer(step)
         remote(q_send.at[to], q_recv.at[me], q_ssem, q_rsem, to).start()
 
     pltpu.make_async_copy(q_send.at[me], q_recv.at[me], q_rsem).start()
-
-    slot_there = lax.rem(me, SPARE)
-
-    def spare_target(index):
-        return SPARE_DEVICES * index + me // SPARE
-
-    def query_copy(index):
-        return remote(
-            q_send.at[BLK + index],
-            q_spare.at[slot_there],
-            q_ssem2.at[index],
-            q_rsem2.at[slot_there],
-            spare_target(index),
-        )
-
-    def state_rows(head):
-        return states_v.at[pl.ds(pl.multiple_of(HD * head, HD), HD)]
-
-    def state_copy(index):
-        return remote(
-            state_rows(BLK + index),
-            state_spare.at[slot_there],
-            state_ssem2.at[index],
-            state_rsem2.at[slot_there],
-            spare_target(index),
-        )
 
     for index in range(SPARE_HEADS):
 
@@ -332,6 +409,24 @@
         def _():
             pltpu.make_async_copy(
                 q_send.at[BLK + index], q_spare.at[slot_there], q_rsem2.at[slot_there]
+            ).start()
+
+    @pl.loop(0, BLK - 1)
+    def _(step):
+        to = peer(step)
+        remote(state_rows(to), state_recv.at[me], state_ssem, state_rsem, to).start()
+
+    pltpu.make_async_copy(state_rows(me), state_recv.at[me], state_rsem).start()
+    for index in range(SPARE_HEADS):
+
+        @pl.when(spare_target(index) != me)
+        def _():
+            state_copy(index).start()
+
+        @pl.when(spare_target(index) == me)
+        def _():
+            pltpu.make_async_copy(
+                state_rows(BLK + index), state_spare.at[slot_there], state_rsem2.at[slot_there]
             ).start()
 
     project(1280, 2432)
@@ -353,96 +448,8 @@
     pack_heads(fresh_v, main_send.at[1], spare_send.at[1])
     send_main(1)
 
-    @pl.loop(1, BLK)
-    def _(step):
-        to = lax.rem(me + step, BLK)
-        remote(state_rows(to), state_recv.at[me], state_ssem, state_rsem, to).start()
-
-    pltpu.make_async_copy(state_rows(me), state_recv.at[me], state_rsem).start()
-    for index in range(SPARE_HEADS):
-
-        @pl.when(spare_target(index) != me)
-        def _():
-            state_copy(index).start()
-
-        @pl.when(spare_target(index) == me)
-        def _():
-            pltpu.make_async_copy(
-                state_rows(BLK + index), state_spare.at[slot_there], state_rsem2.at[slot_there]
-            ).start()
-
     send_spare(0)
     send_spare(1)
-
-    load_text.wait()
-    text_normed = (
-        layer_norm(text_v[...].astype(F32).T) * (1.0 + mod_v[row, 4]) + mod_v[row, 3]
-    ).astype(BF)
-    text_send[...] = (
-        lax.dot_general(
-            text_weight_ref[...],
-            text_normed,
-            (((1,), (1,)), ((), ())),
-            preferred_element_type=F32,
-        )
-        .astype(BF)
-        .astype(F32)
-    )
-
-    def text_main(step):
-        unit = TEXT_COLS // 8 * me + step
-        second = unit // TEXT_COLS
-        head = (unit - TEXT_COLS * second) // 8
-        to_row = pl.multiple_of(HD * second + 8 * lax.rem(unit, 8), 8)
-        source = text_send.at[pl.ds(pl.multiple_of(8 * step, 8), 8)]
-        target = text_recv.at[0, pl.ds(to_row, 8)]
-        return (
-            head,
-            lambda: remote(source, target, text_ssem.at[step], text_rsem.at[0], head),
-            lambda: pltpu.make_async_copy(source, target, text_rsem.at[0]),
-        )
-
-    @pl.loop(0, TEXT_COLS // 8)
-    def _(step):
-        head, away, local = text_main(step)
-
-        @pl.when(jnp.logical_and(head < BLK, head != me))
-        def _():
-            away().start()
-
-        @pl.when(head == me)
-        def _():
-            local().start()
-
-    pieces = ((6, 112, 40, 0, 0), (7, 0, 24, 0, 40), (7, 24, 64, 1, 0), (7, 88, 64, 2, 0))
-    second_half = me // 8
-
-    def text_spare(number, step):
-        _, row, rows, index, to_row = pieces[number]
-        to = SPARE_DEVICES * index + step
-        source = text_send.at[pl.ds(row, rows)]
-        target = text_recv.at[1, pl.ds(pl.multiple_of(HD * second_half + to_row, 8), rows)]
-        return (
-            to,
-            lambda: remote(source, target, text_ssem2.at[number, step], text_rsem.at[1], to),
-            lambda: pltpu.make_async_copy(source, target, text_rsem.at[1]),
-        )
-
-    for number in range(4):
-
-        @pl.when(lax.rem(me, 8) == pieces[number][0])
-        def _():
-            @pl.loop(0, SPARE_DEVICES)
-            def _(step):
-                to, away, local = text_spare(number, step)
-
-                @pl.when(to != me)
-                def _():
-                    away().start()
-
-                @pl.when(to == me)
-                def _():
-                    local().start()
 
     one = jnp.ones((1, 128), F32)
     low1 = low_half(1)
@@ -499,7 +506,9 @@
 
     def text_entries(which):
         arrived(text_recv.at[which], text_rsem.at[which])
-        value = text_recv[which].T
+        tiles = text_recv[which].astype(F32)
+        halves = [tiles[:, 8 * half : 8 * half + 8].reshape(128, 128) for half in range(2)]
+        value = jnp.concatenate([halves[0].T, halves[1].T], axis=0)
         square = jnp.where(low256, value * value, 0.0)
         mean = jnp.sum(square, axis=1, keepdims=True) * (1.0 / HD)
         scaled = value * lax.rsqrt(mean + 1e-06) * text_gain
@@ -519,7 +528,8 @@
         target = out_hbm.at[pl.ds(pl.multiple_of(HD * head, HD), HD)]
         return remote(out_send.at[slot], target, sem, out_rsem, block, after)
 
-    def finish(step):
+    def finish(turn):
+        step = lax.rem(me + turn, ROWS // QT)
         acc[query_rows(step)] += attend(query_rows(step), fresh_entries, fresh_values)
         for part in range(QT // TOK):
             block = step * (QT // TOK) + part
@@ -529,20 +539,18 @@
             result_copy(block, me, block, out_ssem).start()
 
     arrived(state_recv, state_rsem)
+    pl.loop(0, 2)(finish)
     pass_spare(0)
-    finish(0)
+    pl.loop(2, ROWS // QT)(finish)
     pass_spare(1)
-    pl.loop(1, ROWS // QT)(finish)
 
     @pl.when(has_spare)
     def _():
         spare_recv[1, BLK : BLK + 2] = text_entries(1)
-        for kind in range(2):
-            arrived(spare_recv.at[kind, pl.ds(8 * (1 - core), 8)], pass_rsem.at[kind])
-            pass_copy(kind).wait_send()
         rows = pl.ds(ROWS, SPARE_ROWS)
         total = jnp.zeros((SPARE_ROWS, 128), F32)
         for kind, tiles in ((0, BLK), (1, BLK + 2)):
+            arrived(spare_recv.at[kind, pl.ds(8 * (1 - core), 8)], pass_rsem.at[kind])
             entries = spare_recv[kind, 0:tiles].reshape(tiles * TOK, 128)
             total = total + attend(rows, entries, with_ones(entries))
         acc[rows] = total
@@ -604,17 +612,26 @@
             result_copy(
                 BLK + slot, BLK + spare_index, first_block + slot, out_ssem2.at[slot]
             ).wait_send()
-
-
-def write_results(raw_states, raw_fresh, states_out, fresh_out, sems):
-    copies = (
-        pltpu.make_async_copy(raw_states, states_out, sems.at[0]),
-        pltpu.make_async_copy(raw_fresh, fresh_out, sems.at[1]),
+        for kind in range(2):
+            pass_copy(kind).wait_send()
+
+
+def write_results(raw_states, raw_fresh, states_out, fresh_out, states_v, fresh_v, sems):
+    loads = (
+        pltpu.make_async_copy(raw_fresh, fresh_v, sems.at[0]),
+        pltpu.make_async_copy(raw_states, states_v, sems.at[1]),
     )
-    for copy in copies:
-        copy.start()
-    for copy in copies:
-        copy.wait()
+    stores = (
+        pltpu.make_async_copy(fresh_v, fresh_out, sems.at[0]),
+        pltpu.make_async_copy(states_v, states_out, sems.at[1]),
+    )
+    for load in loads:
+        load.start()
+    for load, store in zip(loads, stores):
+        load.wait()
+        store.start()
+    for store in stores:
+        store.wait()
 
 
 def body(
@@ -674,8 +691,8 @@
             pltpu.VMEM((BLK, HD, 128), BF),
             pltpu.VMEM((SPARE, HD, 128), BF),
             pltpu.VMEM((ROWS + SPARE_ROWS, 128), F32),
-            pltpu.VMEM((TEXT_COLS, TEXT), F32),
-            pltpu.VMEM((2, 128, TEXT), F32),
+            pltpu.VMEM((TEXT_COLS // 8, 16, 128), BF),
+            pltpu.VMEM((2, 16, 16, 128), BF),
             pltpu.VMEM((24, 128), F32),
             pltpu.VMEM((BLK + SPARE, HD, 128), BF),
             dma((4,)),
@@ -726,7 +743,7 @@
         ),
         in_specs=[anywhere, anywhere],
         out_specs=(anywhere, anywhere),
-        scratch_shapes=[dma((2,))],
+        scratch_shapes=[pltpu.VMEM((D, TOK), BF), pltpu.VMEM((TOK, 2 * D), BF), dma((2,))],
         compiler_params=pltpu.CompilerParams(vmem_limit_bytes=60 * 1024 * 1024),
     )(next_states, fresh)
     return (jnp.swapaxes(next_states, 0, 1)[None], fresh[None])

time: 93 us -> 61.9 us (0.67)
  Pallas kernels: 90.8 us -> 59.6 us
    pallas_call x1, Pallas kernels: 29.4 us -> 2.02 us  [body(): pl.pallas_call(write_results, out_shape=(jax.ShapeDtypeStruct((D, TOK), B...]
    pallas_call x1, Pallas kernels: 61.4 us -> 57.6 us  [body(): pl.pallas_call(functools.partial(kernel, sections), out_shape=(jax.ShapeD...]
where the time goes in v4:
time: 61.9 us; the launch traced here: 61.7 us
  Pallas kernels  59.6 us (96%)
  between operations  2.09 us (3%)
    pallas_call x1, Pallas kernels, body(): pl.pallas_call(functools.partial(kernel, sections), out_shape=(jax.ShapeD...  57.6 us
    pallas_call x1, Pallas kernels, body(): pl.pallas_call(write_results, out_shape=(jax.ShapeDtypeStruct((D, TOK), B...  2.02 us

profile of v4, /device:TPU:1, one launch (start us, length us, event | category | flops | bytes accessed | tf_op | source)
XLA Modules:
  0.0 61.7 jit_solution(16922369794036674367)
XLA Ops:
  1.9 57.6 %shard_map.122 = (bf16[1216,128]{1,0:T(8,128)(2,1)}, bf16[128,2432]{1,0:T(8,128)(2,1)}) custom-call(s32[1]{0:T(128)S(6)} %copy.14.patch_ref, s32[1]{0:T(128)S(6)} %copy.13.step_ref, bf16[1216,128]{1,0:T(8,128)(2,1)} %bitcast.21, bf16[1216,3648]{1,0:T(8,128)(2,1)} %bitcast.16, bf16[152,1216]{1,0:T(8,128)(2,1)} %bitcast.20, bf16[1216,256]{1,0:T(8,128)(2,1)} %bitcast.19, ...), custom_call_target="tpu_custom_call" | custom-call | tf_op jit(solution)/shard_map/pallas_call | solution.py:654
  59.5 2.0 %shard_map.123 = (bf16[1216,128]{1,0:T(8,128)(2,1)}, bf16[128,2432]{1,0:T(8,128)(2,1)}) custom-call(bf16[1216,128]{1,0:T(8,128)(2,1)} %get-tuple-element.6.raw_states, bf16[128,2432]{1,0:T(8,128)(2,1)} %get-tuple-element.7.raw_fresh), custom_call_target="tpu_custom_call" | custom-call | tf_op jit(solution)/shard_map/pallas_call | solution.py:738

commit v5 on v4

--- a/solution.py
+++ b/solution.py
@@ -82,15 +82,13 @@
     proj_v,
     fresh_v,
     main_send,
-    main_recv,
+    kv,
     spare_send,
-    spare_recv,
     q_send,
     q_recv,
     q_spare,
     q_all,
     state_recv,
-    state_spare,
     acc,
     text_send,
     text_recv,
@@ -113,10 +111,8 @@
     state_ssem2,
     state_rsem2,
     text_ssem,
-    text_ssem2,
     text_rsem,
     out_ssem,
-    out_ssem2,
     out_rsem,
     fresh_sem,
 ):
@@ -158,10 +154,12 @@
     core = lax.rem(me, 2)
     chip = me // 2
     sibling = me + 1 - 2 * core
-    spare_index = me // SPARE_DEVICES
+    spare_index = lax.rem(chip, 4)
     has_spare = spare_index < SPARE_HEADS
-    first_block = SPARE * lax.rem(me, SPARE_DEVICES)
-    SPARE_CHIPS = SPARE_HEADS * SPARE_DEVICES // 2
+    first_block = SPARE * (2 * (me // 8) + core)
+
+    def spare_device(index, part):
+        return 8 * (part // 2) + 2 * index + lax.rem(part, 2)
 
     def peer(step):
         ring = step // 4
@@ -191,20 +189,20 @@
             to = peer(step)
             remote(
                 main_send.at[kind, to],
-                main_recv.at[kind, me],
+                kv.at[0, kind, me],
                 main_ssem.at[kind],
                 main_rsem.at[kind],
                 to,
             ).start()
 
         pltpu.make_async_copy(
-            main_send.at[kind, me], main_recv.at[kind, me], main_rsem.at[kind]
+            main_send.at[kind, me], kv.at[0, kind, me], main_rsem.at[kind]
         ).start()
 
     def spare_copy(kind, to_chip):
         return remote(
-            spare_send.at[kind, 2 * to_chip // SPARE_DEVICES],
-            spare_recv.at[kind, 8 * core + chip],
+            spare_send.at[kind, lax.rem(to_chip, 4)],
+            kv.at[1, kind, 8 * core + chip],
             spare_ssem.at[kind, to_chip],
             spare_rsem.at[kind],
             2 * to_chip + core,
@@ -215,7 +213,7 @@
         def _(step):
             to_chip = peer(2 * step) // 2
 
-            @pl.when(jnp.logical_and(to_chip != chip, to_chip < SPARE_CHIPS))
+            @pl.when(jnp.logical_and(to_chip != chip, lax.rem(to_chip, 4) < SPARE_HEADS))
             def _():
                 spare_copy(kind, to_chip).start()
 
@@ -223,18 +221,18 @@
         def _():
             pltpu.make_async_copy(
                 spare_send.at[kind, spare_index],
-                spare_recv.at[kind, 8 * core + chip],
+                kv.at[1, kind, 8 * core + chip],
                 spare_rsem.at[kind],
             ).start()
 
     def pass_copy(kind):
-        block = spare_recv.at[kind, pl.ds(8 * core, 8)]
+        block = kv.at[1, kind, pl.ds(8 * core, 8)]
         return remote(block, block, pass_ssem.at[kind], pass_rsem.at[kind], sibling)
 
     def pass_spare(kind):
         @pl.when(has_spare)
         def _():
-            arrived(spare_recv.at[kind, pl.ds(8 * core, 8)], spare_rsem.at[kind])
+            arrived(kv.at[1, kind, pl.ds(8 * core, 8)], spare_rsem.at[kind])
             pass_copy(kind).start()
 
     load_stale.wait()
@@ -262,64 +260,58 @@
         eight = text_part[8 * unit : 8 * unit + 8]
         text_send[unit] = jnp.concatenate([eight[:, :128], eight[:, 128:]], axis=0).astype(BF)
 
-    def text_main(step):
-        unit = TEXT_COLS // 8 * me + step
-        second = unit // TEXT_COLS
-        head = (unit - TEXT_COLS * second) // 8
-        source = text_send.at[step]
-        target = text_recv.at[0, 8 * second + lax.rem(unit, 8)]
-        return (
-            head,
-            lambda: remote(source, target, text_ssem.at[step], text_rsem.at[0], head),
-            lambda: pltpu.make_async_copy(source, target, text_rsem.at[0]),
-        )
-
-    @pl.loop(0, TEXT_COLS // 8)
-    def _(step):
-        head, away, local = text_main(step)
-
-        @pl.when(jnp.logical_and(head < BLK, head != me))
-        def _():
-            away().start()
-
-        @pl.when(head == me)
-        def _():
-            local().start()
-
-    pieces = ((6, 14, 5, 0, 0), (7, 0, 3, 0, 5), (7, 3, 8, 1, 0), (7, 11, 8, 2, 0))
     second_half = me // 8
-
-    def text_spare(number, step):
-        _, row, rows, index, to_row = pieces[number]
-        to = SPARE_DEVICES * index + step
-        source = text_send.at[pl.ds(row, rows)]
-        target = text_recv.at[1, pl.ds(8 * second_half + to_row, rows)]
-        return (
-            to,
-            lambda: remote(source, target, text_ssem2.at[number, step], text_rsem.at[1], to),
-            lambda: pltpu.make_async_copy(source, target, text_rsem.at[1]),
-        )
-
-    for number in range(4):
-
-        @pl.when(lax.rem(me, 8) == pieces[number][0])
-        def _():
-            @pl.loop(0, SPARE_DEVICES)
-            def _(step):
-                to, away, local = text_spare(number, step)
-
-                @pl.when(to != me)
-                def _():
-                    away().start()
-
-                @pl.when(to == me)
-                def _():
-                    local().start()
+    half_units = TEXT_COLS // 8
+
+    def text_pieces(place):
+        pieces = []
+        unit = half_units * place
+        while unit < half_units * (place + 1):
+            head = unit // 8
+            end = min(8 * head + 8, half_units * (place + 1))
+            pieces.append((unit - half_units * place, end - unit, head, unit % 8))
+            unit = end
+        return pieces
+
+    def text_copies(act, act_local):
+        for place in range(8):
+
+            @pl.when(lax.rem(me, 8) == place)
+            def _():
+                for number, (row, units, head, to_row) in enumerate(text_pieces(place)):
+                    spare = head >= BLK
+                    source = text_send.at[pl.ds(row, units)]
+                    target = text_recv.at[int(spare), pl.ds(8 * second_half + to_row, units)]
+
+                    @pl.loop(0, SPARE_DEVICES if spare else 1)
+                    def _(step):
+                        to = spare_device(head - BLK, step) if spare else jnp.int32(head)
+
+                        @pl.when(to != me)
+                        def _():
+                            act(
+                                remote(
+                                    source,
+                                    target,
+                                    text_ssem.at[number, step],
+                                    text_rsem.at[int(spare)],
+                                    to,
+                                )
+                            )
+
+                        @pl.when(to == me)
+                        def _():
+                            act_local(source, target, text_rsem.at[int(spare)])
+
+    text_copies(
+        lambda copy: copy.start(),
+        lambda source, target, sem: pltpu.make_async_copy(source, target, sem).start(),
+    )
 
     slot_there = lax.rem(me, SPARE)
 
     def spare_target(index):
-        return SPARE_DEVICES * index + me // SPARE
+        return spare_device(index, me // SPARE)
 
     def query_copy(index):
         return remote(
@@ -336,7 +328,7 @@
     def state_copy(index):
         return remote(
             state_rows(BLK + index),
-            state_spare.at[slot_there],
+            state_recv.at[BLK + slot_there],
             state_ssem2.at[index],
             state_rsem2.at[slot_there],
             spare_target(index),
@@ -426,7 +418,7 @@
         @pl.when(spare_target(index) == me)
         def _():
             pltpu.make_async_copy(
-                state_rows(BLK + index), state_spare.at[slot_there], state_rsem2.at[slot_there]
+                state_rows(BLK + index), state_recv.at[BLK + slot_there], state_rsem2.at[slot_there]
             ).start()
 
     project(1280, 2432)
@@ -490,21 +482,10 @@
         powers = jnp.exp(scores).astype(BF)
         return jnp.dot(powers, values, preferred_element_type=F32)
 
-    def query_rows(step):
-        return pl.ds(pl.multiple_of(step * QT, QT), QT)
-
-    arrived(main_recv.at[0, pl.ds(0, BLK)], main_rsem.at[0])
-    stale_entries = main_recv[0, 0:BLK].reshape(BLK * TOK, 128)
-    stale_values = with_ones(stale_entries)
-
-    @pl.loop(0, ROWS // QT)
-    def _(step):
-        acc[query_rows(step)] = attend(query_rows(step), stale_entries, stale_values)
-
     low256 = low_half(TEXT)
     text_gain = jnp.concatenate([text_gain_ref[...], jnp.ones((1, HD), F32)], axis=1)
 
-    def text_entries(which):
+    def take_text(which):
         arrived(text_recv.at[which], text_rsem.at[which])
         tiles = text_recv[which].astype(F32)
         halves = [tiles[:, 8 * half : 8 * half + 8].reshape(128, 128) for half in range(2)]
@@ -512,56 +493,77 @@
         square = jnp.where(low256, value * value, 0.0)
         mean = jnp.sum(square, axis=1, keepdims=True) * (1.0 / HD)
         scaled = value * lax.rsqrt(mean + 1e-06) * text_gain
-        return jnp.where(low256, scaled, value).astype(BF).reshape(2, TOK, 128)
-
-    main_recv[1, BLK : BLK + 2] = text_entries(0)
-    arrived(main_recv.at[1, pl.ds(0, BLK)], main_rsem.at[1])
-    fresh_entries = main_recv[1].reshape((BLK + 2) * TOK, 128)
-    fresh_values = with_ones(fresh_entries)
-
-    def result_of(row, head, states):
-        value = acc[pl.ds(row, TOK)] * gate_v[pl.ds(head, 1), :]
-        turned = value.T
-        return (states.astype(F32) + turned[HD:] / turned[:HD]).astype(BF)
-
-    def result_copy(slot, head, block, sem):
-        target = out_hbm.at[pl.ds(pl.multiple_of(HD * head, HD), HD)]
-        return remote(out_send.at[slot], target, sem, out_rsem, block, after)
-
-    def finish(turn):
-        step = lax.rem(me + turn, ROWS // QT)
-        acc[query_rows(step)] += attend(query_rows(step), fresh_entries, fresh_values)
-        for part in range(QT // TOK):
-            block = step * (QT // TOK) + part
-            out_send[block] = result_of(
-                pl.multiple_of(block * TOK, TOK), me, state_recv[block]
-            )
-            result_copy(block, me, block, out_ssem).start()
-
-    arrived(state_recv, state_rsem)
-    pl.loop(0, 2)(finish)
-    pass_spare(0)
-    pl.loop(2, ROWS // QT)(finish)
-    pass_spare(1)
+        entries = jnp.where(low256, scaled, value).astype(BF)
+        kv[which, 0, BLK] = entries[:TOK]
+        kv[which, 1, BLK] = entries[TOK:]
+
+    take_text(0)
 
     @pl.when(has_spare)
     def _():
-        spare_recv[1, BLK : BLK + 2] = text_entries(1)
-        rows = pl.ds(ROWS, SPARE_ROWS)
-        total = jnp.zeros((SPARE_ROWS, 128), F32)
-        for kind, tiles in ((0, BLK), (1, BLK + 2)):
-            arrived(spare_recv.at[kind, pl.ds(8 * (1 - core), 8)], pass_rsem.at[kind])
-            entries = spare_recv[kind, 0:tiles].reshape(tiles * TOK, 128)
-            total = total + attend(rows, entries, with_ones(entries))
-        acc[rows] = total
-        for slot in range(SPARE):
-            arrived(state_spare.at[slot], state_rsem2.at[slot])
-            out_send[BLK + slot] = result_of(
-                ROWS + slot * TOK, BLK + spare_index, state_spare[slot]
-            )
-            result_copy(
-                BLK + slot, BLK + spare_index, first_block + slot, out_ssem2.at[slot]
-            ).start()
+        take_text(1)
+
+    acc[...] = jnp.zeros_like(acc)
+    arrived(kv.at[0, 0, pl.ds(0, BLK)], main_rsem.at[0])
+
+    tiles = ROWS // QT
+    per_tile = QT // TOK
+
+    def result_copy(slot):
+        main = slot < BLK
+        head = jnp.where(main, me, BLK + spare_index)
+        target = out_hbm.at[pl.ds(pl.multiple_of(HD * head, HD), HD)]
+        block = jnp.where(main, slot, first_block + slot - BLK)
+        return remote(out_send.at[slot], target, out_ssem.at[slot], out_rsem, block, after)
+
+    @pl.loop(0, 2 * tiles + 2)
+    def _(item):
+        @pl.when(item == tiles)
+        def _():
+            arrived(kv.at[0, 1, pl.ds(0, BLK)], main_rsem.at[1])
+            arrived(state_recv.at[pl.ds(0, BLK)], state_rsem)
+
+        @pl.when(item == tiles + 2)
+        def _():
+            pass_spare(0)
+
+        @pl.when(item == 2 * tiles)
+        def _():
+            pass_spare(1)
+
+        main = item < 2 * tiles
+        kind = jnp.where(main, item // tiles, item - 2 * tiles)
+        which = jnp.where(main, 0, 1)
+        step = jnp.where(main, lax.rem(me + item, tiles), tiles)
+
+        @pl.when(jnp.logical_and(has_spare, jnp.logical_not(main)))
+        def _():
+            arrived(kv.at[1, kind, pl.ds(8 * (1 - core), 8)], pass_rsem.at[kind])
+
+        @pl.when(jnp.logical_or(has_spare, main))
+        def _():
+            rows = pl.ds(pl.multiple_of(step * QT, QT), QT)
+            entries = kv[which, kind].reshape((BLK + 1) * TOK, 128)
+            acc[rows] += attend(rows, entries, with_ones(entries))
+
+        @pl.when(jnp.logical_and(has_spare, item == 2 * tiles + 1))
+        def _():
+            for slot in range(SPARE):
+                arrived(state_recv.at[BLK + slot], state_rsem2.at[slot])
+
+        @pl.when(jnp.logical_and(kind == 1, jnp.logical_or(has_spare, main)))
+        def _():
+            gate = gate_v[pl.ds(jnp.where(main, me, BLK + spare_index), 1), :]
+
+            @pl.loop(0, per_tile)
+            def _(part):
+                slot = step * per_tile + part
+                value = acc[pl.ds(pl.multiple_of(slot * TOK, TOK), TOK)] * gate
+                turned = value.T
+                out_send[slot] = (
+                    state_recv[slot].astype(F32) + turned[HD:] / turned[:HD]
+                ).astype(BF)
+                result_copy(slot).start()
 
     arrived(out_hbm, out_rsem)
 
@@ -569,9 +571,9 @@
     for kind in range(2):
         arrived(main_send.at[kind, pl.ds(0, BLK - 1)], main_ssem.at[kind])
 
-        @pl.loop(0, SPARE_CHIPS)
+        @pl.loop(0, BLK // 2)
         def _(to_chip):
-            @pl.when(to_chip != chip)
+            @pl.when(jnp.logical_and(to_chip != chip, lax.rem(to_chip, 4) < SPARE_HEADS))
             def _():
                 spare_copy(kind, to_chip).wait_send()
 
@@ -584,34 +586,16 @@
             query_copy(index).wait_send()
             state_copy(index).wait_send()
 
-    @pl.loop(0, TEXT_COLS // 8)
-    def _(step):
-        head, away, _ = text_main(step)
-
-        @pl.when(jnp.logical_and(head < BLK, head != me))
-        def _():
-            away().wait_send()
-
-    for number in range(4):
-
-        @pl.when(lax.rem(me, 8) == pieces[number][0])
-        def _():
-            @pl.loop(0, SPARE_DEVICES)
-            def _(step):
-                to, away, _ = text_spare(number, step)
-
-                @pl.when(to != me)
-                def _():
-                    away().wait_send()
-
-    arrived(out_send.at[pl.ds(0, BLK)], out_ssem)
+    text_copies(lambda copy: copy.wait_send(), lambda *_: None)
+
+    @pl.loop(0, BLK)
+    def _(slot):
+        result_copy(slot).wait_send()
 
     @pl.when(has_spare)
     def _():
         for slot in range(SPARE):
-            result_copy(
-                BLK + slot, BLK + spare_index, first_block + slot, out_ssem2.at[slot]
-            ).wait_send()
+            result_copy(BLK + slot).wait_send()
         for kind in range(2):
             pass_copy(kind).wait_send()
 
@@ -681,15 +665,13 @@
             pltpu.VMEM((TOK, 3 * D + 64), F32),
             pltpu.VMEM((TOK, 2 * D), BF),
             pltpu.VMEM((2, BLK, TOK, 128), BF),
-            pltpu.VMEM((2, BLK + 2, TOK, 128), BF),
+            pltpu.VMEM((2, 2, BLK + 1, TOK, 128), BF),
             pltpu.VMEM((2, SPARE_HEADS, TOK, 128), BF),
-            pltpu.VMEM((2, BLK + 2, TOK, 128), BF),
             pltpu.VMEM((HEADS, HD, 128), BF),
             pltpu.VMEM((BLK, HD, 128), BF),
             pltpu.VMEM((SPARE, HD, 128), BF),
             pltpu.VMEM((ROWS + SPARE_ROWS, 128), BF),
-            pltpu.VMEM((BLK, HD, 128), BF),
-            pltpu.VMEM((SPARE, HD, 128), BF),
+            pltpu.VMEM((BLK + SPARE, HD, 128), BF),
             pltpu.VMEM((ROWS + SPARE_ROWS, 128), F32),
             pltpu.VMEM((TEXT_COLS // 8, 16, 128), BF),
             pltpu.VMEM((2, 16, 16, 128), BF),
@@ -711,11 +693,9 @@
             dma,
             dma((SPARE_HEADS,)),
             dma((SPARE,)),
-            dma((TEXT_COLS // 8,)),
             dma((4, SPARE_DEVICES)),
             dma((2,)),
-            dma,
-            dma((SPARE,)),
+            dma((BLK + SPARE,)),
             dma,
             dma,
         ],

time: 61.9 us -> 59.9 us (0.968)
  Pallas kernels: 59.6 us -> 57.8 us
    pallas_call x1, Pallas kernels: 57.6 us -> 55.8 us  [body(): pl.pallas_call(functools.partial(kernel, sections), out_shape=(jax.ShapeD...]
where the time goes in v5:
time: 59.9 us; the launch traced here: 59.7 us
  Pallas kernels  57.8 us (96%)
  between operations  1.93 us (3%)
    pallas_call x1, Pallas kernels, body(): pl.pallas_call(functools.partial(kernel, sections), out_shape=(jax.ShapeD...  55.8 us
    pallas_call x1, Pallas kernels, body(): pl.pallas_call(write_results, out_shape=(jax.ShapeDtypeStruct((D, TOK), B...  2.02 us

profile of v5, /device:TPU:1, one launch (start us, length us, event | category | flops | bytes accessed | tf_op | source)
XLA Modules:
  0.0 59.7 jit_solution(13015050799825921127)
XLA Ops:
  1.9 55.8 %shard_map.122 = (bf16[1216,128]{1,0:T(8,128)(2,1)}, bf16[128,2432]{1,0:T(8,128)(2,1)}) custom-call(s32[1]{0:T(128)S(6)} %copy.14.patch_ref, s32[1]{0:T(128)S(6)} %copy.13.step_ref, bf16[1216,128]{1,0:T(8,128)(2,1)} %bitcast.21, bf16[1216,3648]{1,0:T(8,128)(2,1)} %bitcast.16, bf16[152,1216]{1,0:T(8,128)(2,1)} %bitcast.20, bf16[1216,256]{1,0:T(8,128)(2,1)} %bitcast.19, ...), custom_call_target="tpu_custom_call" | custom-call | tf_op jit(solution)/shard_map/pallas_call | solution.py:638
  57.7 2.0 %shard_map.123 = (bf16[1216,128]{1,0:T(8,128)(2,1)}, bf16[128,2432]{1,0:T(8,128)(2,1)}) custom-call(bf16[1216,128]{1,0:T(8,128)(2,1)} %get-tuple-element.6.raw_states, bf16[128,2432]{1,0:T(8,128)(2,1)} %get-tuple-element.7.raw_fresh), custom_call_target="tpu_custom_call" | custom-call | tf_op jit(solution)/shard_map/pallas_call | solution.py:718

commit v6 on v5

--- a/solution.py
+++ b/solution.py
@@ -523,11 +523,11 @@
             arrived(kv.at[0, 1, pl.ds(0, BLK)], main_rsem.at[1])
             arrived(state_recv.at[pl.ds(0, BLK)], state_rsem)
 
-        @pl.when(item == tiles + 2)
+        @pl.when(item == tiles + 1)
         def _():
             pass_spare(0)
 
-        @pl.when(item == 2 * tiles)
+        @pl.when(item == 2 * tiles - 1)
         def _():
             pass_spare(1)
 

time: 59.9 us -> 59.4 us (level)
  no operation moved by 1% of the time
where the time goes in v6:
time: 59.4 us; the launch traced here: 59.3 us
  Pallas kernels  57.3 us (96%)
  between operations  1.93 us (3%)
    pallas_call x1, Pallas kernels, body(): pl.pallas_call(functools.partial(kernel, sections), out_shape=(jax.ShapeD...  55.3 us
    pallas_call x1, Pallas kernels, body(): pl.pallas_call(write_results, out_shape=(jax.ShapeDtypeStruct((D, TOK), B...  2.02 us

profile of v6, /device:TPU:1, one launch (start us, length us, event | category | flops | bytes accessed | tf_op | source)
XLA Modules:
  0.0 59.3 jit_solution(16367677080559035001)
XLA Ops:
  1.9 55.3 %shard_map.122 = (bf16[1216,128]{1,0:T(8,128)(2,1)}, bf16[128,2432]{1,0:T(8,128)(2,1)}) custom-call(s32[1]{0:T(128)S(6)} %copy.14.patch_ref, s32[1]{0:T(128)S(6)} %copy.13.step_ref, bf16[1216,128]{1,0:T(8,128)(2,1)} %bitcast.21, bf16[1216,3648]{1,0:T(8,128)(2,1)} %bitcast.16, bf16[152,1216]{1,0:T(8,128)(2,1)} %bitcast.20, bf16[1216,256]{1,0:T(8,128)(2,1)} %bitcast.19, ...), custom_call_target="tpu_custom_call" | custom-call | tf_op jit(solution)/shard_map/pallas_call | solution.py:638
  57.2 2.0 %shard_map.123 = (bf16[1216,128]{1,0:T(8,128)(2,1)}, bf16[128,2432]{1,0:T(8,128)(2,1)}) custom-call(bf16[1216,128]{1,0:T(8,128)(2,1)} %get-tuple-element.6.raw_states, bf16[128,2432]{1,0:T(8,128)(2,1)} %get-tuple-element.7.raw_fresh), custom_call_target="tpu_custom_call" | custom-call | tf_op jit(solution)/shard_map/pallas_call | solution.py:718

commit v7 on v6

--- a/solution.py
+++ b/solution.py
@@ -556,7 +556,8 @@
             gate = gate_v[pl.ds(jnp.where(main, me, BLK + spare_index), 1), :]
 
             @pl.loop(0, per_tile)
-            def _(part):
+            def _(turn):
+                part = lax.rem(turn + me // per_tile, per_tile)
                 slot = step * per_tile + part
                 value = acc[pl.ds(pl.multiple_of(slot * TOK, TOK), TOK)] * gate
                 turned = value.T

time: 59.4 us -> 59.1 us (level)
  no operation moved by 1% of the time
where the time goes in v7:
time: 59.1 us; the launch traced here: 58.9 us
  Pallas kernels  57 us (96%)
  between operations  1.93 us (3%)
    pallas_call x1, Pallas kernels, body(): pl.pallas_call(functools.partial(kernel, sections), out_shape=(jax.ShapeD...  55 us
    pallas_call x1, Pallas kernels, body(): pl.pallas_call(write_results, out_shape=(jax.ShapeDtypeStruct((D, TOK), B...  2.02 us

profile of v7, /device:TPU:1, one launch (start us, length us, event | category | flops | bytes accessed | tf_op | source)
XLA Modules:
  0.0 58.9 jit_solution(5635612806463626538)
XLA Ops:
  1.9 55.0 %shard_map.122 = (bf16[1216,128]{1,0:T(8,128)(2,1)}, bf16[128,2432]{1,0:T(8,128)(2,1)}) custom-call(s32[1]{0:T(128)S(6)} %copy.14.patch_ref, s32[1]{0:T(128)S(6)} %copy.13.step_ref, bf16[1216,128]{1,0:T(8,128)(2,1)} %bitcast.21, bf16[1216,3648]{1,0:T(8,128)(2,1)} %bitcast.16, bf16[152,1216]{1,0:T(8,128)(2,1)} %bitcast.20, bf16[1216,256]{1,0:T(8,128)(2,1)} %bitcast.19, ...), custom_call_target="tpu_custom_call" | custom-call | tf_op jit(solution)/shard_map/pallas_call | solution.py:639
  56.9 2.0 %shard_map.123 = (bf16[1216,128]{1,0:T(8,128)(2,1)}, bf16[128,2432]{1,0:T(8,128)(2,1)}) custom-call(bf16[1216,128]{1,0:T(8,128)(2,1)} %get-tuple-element.6.raw_states, bf16[128,2432]{1,0:T(8,128)(2,1)} %get-tuple-element.7.raw_fresh), custom_call_target="tpu_custom_call" | custom-call | tf_op jit(solution)/shard_map/pallas_call | solution.py:719
